TPU v7x, 128 devices: a whole 4x4x4 slice. The times are simulated.
128 devices in a mesh: section: 8 (over y_hi, x), dp: 16 (over z, y_lo, core).
Axes of the slice: x: 4, y: 4 (y_hi: 2, y_lo: 2; y = y_hi * 2 + y_lo), z: 4, core: 2. Of those that a mesh axis runs over, the one named last changes fastest.
Arguments:
- tokens: bfloat16 [2, 2048, 2048], P(None, 'dp'), may hold values from -12 to 12
- cotangent: bfloat16 [2, 2048, 2048], P(None, 'dp'), may hold values from -12 to 12
- gain: float32 [8, 2048], P('section'), may hold values from 0.3 to 3
- weight: bfloat16 [16384, 2048], P('section'), may hold values from -0.125 to 0.125
Outputs:
- act_roots: float32 [8192, 2048], P(('section', 'dp'))
- grad_roots: float32 [8192, 2048], P(('section', 'dp'))
All inputs are finite; a program needn't handle non-finite values. Where the computation divides by a largest or mean magnitude, that divisor is 1e-20 or more.
Results may differ from a plain program's by a relative error of at most 0.00085.
Values may be sent and summed in bfloat16 or wider, within the bound.
A program may use at most 128 MiB of HBM per device.

v0:
```python
import jax
import jax.numpy as jnp
from jax import lax
from jax.sharding import PartitionSpec as P

BLK = 1024


damping_term = 4.0


def shifted(value, axis, steps):
    count = lax.axis_size(axis)
    leading, last = (max(0, -steps), min(count, count - steps))
    return lax.ppermute(value, axis, [(source, source + steps) for source in range(leading, last)])


def gelu_tanh(values):
    return jax.nn.gelu(values, approximate=True)


def layer_forward(inputs, scale_row, matrix):
    widened = inputs.astype(jnp.float32)
    inverse_rms = lax.rsqrt(jnp.mean(widened * widened, axis=-1, keepdims=True) + 1e-06)
    normed = (widened * inverse_rms * scale_row).astype(jnp.bfloat16)
    preact = jnp.dot(normed, matrix, preferred_element_type=jnp.float32)
    outputs = (widened + gelu_tanh(preact)).astype(jnp.bfloat16)
    return (normed, preact, outputs)


def layer_backward(inputs, preact, upstream, scale_row, matrix):
    widened = inputs.astype(jnp.float32)
    inverse_rms = lax.rsqrt(jnp.mean(widened * widened, axis=-1, keepdims=True) + 1e-06)
    upward = upstream.astype(jnp.float32)
    pullback = jax.vjp(gelu_tanh, preact)[1]
    deltas = pullback(upward)[0].astype(jnp.bfloat16)
    backprop = lax.dot_general(
        deltas, matrix, (((1,), (1,)), ((), ())), preferred_element_type=jnp.float32
    )
    normal_hat = widened * inverse_rms
    scaled = backprop * scale_row
    downward = upward + inverse_rms * (
        scaled - normal_hat * jnp.mean(scaled * normal_hat, axis=-1, keepdims=True)
    )
    return (deltas, downward.astype(jnp.bfloat16))


def block_grams(matrix_rows, nblocks):
    split_rows = matrix_rows.reshape(matrix_rows.shape[0], nblocks, BLK)
    return jnp.einsum("rbi,rbj->bij", split_rows, split_rows, preferred_element_type=jnp.float32)


def pack_pairs(partial_value):
    pairs = partial_value.reshape(partial_value.shape[0] // 2, 2, BLK, BLK)
    return (pairs[:, 0], pairs[:, 1])


def unpack_pairs(first_part, second_part):
    even_blocks, odd_blocks = (first_part, second_part)
    return jnp.stack([even_blocks, odd_blocks], axis=1).reshape(-1, BLK, BLK)


def root_rows(summed, row_total, start, count):
    highest = lax.Precision.HIGHEST
    identity = jnp.eye(BLK, dtype=jnp.float32)
    damped = summed / row_total + damping_term * identity
    row_bound = jnp.max(jnp.sum(jnp.abs(damped), axis=2), axis=1)[:, None, None]
    scaled_start = damped / row_bound
    first_step = 1.5 * identity - 0.5 * scaled_start
    start_rows = lax.dynamic_slice_in_dim(scaled_start, start, count, 1)
    identity_rows = lax.dynamic_slice_in_dim(identity, start, count, 0)
    middle = jnp.einsum("bij,bjk->bik", start_rows, first_step, precision=highest)
    square = jnp.einsum("bij,bjk->bik", middle, first_step, precision=highest)
    second = 1.5 * identity_rows - 0.5 * square
    result = jnp.einsum("bij,bjk->bik", second, first_step, precision=highest)
    return jnp.swapaxes(result, 0, 1).reshape(count, -1)


def shards(tokens, cotangent, gain, weight):
    sections = lax.axis_size("section")
    section_index = lax.axis_index("section")
    micro_count, row_count, feature_count = tokens.shape
    nblocks = feature_count // BLK
    scale_row = gain[0]
    row_total = micro_count * row_count * lax.axis_size("dp")
    tick_count = sections + micro_count - 1

    def forward_tick(tick_number, loop_state):
        received, input_store, preact_store, act_partial = loop_state
        micro_slot = tick_number - section_index
        is_active = (micro_slot >= 0) & (micro_slot < micro_count)
        safe_slot = jnp.clip(micro_slot, 0, micro_count - 1)
        fresh_rows = lax.dynamic_index_in_dim(tokens, safe_slot, 0, keepdims=False)
        inputs = jnp.where(section_index == 0, fresh_rows, received)

        def forward_active(operands):
            inputs, input_store, preact_store, act_partial = operands
            normed, preact, outputs = layer_forward(inputs, scale_row, weight)
            input_store = lax.dynamic_update_index_in_dim(input_store, inputs, safe_slot, 0)
            preact_store = lax.dynamic_update_index_in_dim(preact_store, preact, safe_slot, 0)
            return (outputs, input_store, preact_store, act_partial + block_grams(normed, nblocks))

        def forward_resting(operands):
            return (jnp.zeros_like(operands[0]), operands[1], operands[2], operands[3])

        outputs, input_store, preact_store, act_partial = lax.cond(
            is_active,
            forward_active,
            forward_resting,
            (inputs, input_store, preact_store, act_partial),
        )
        received = shifted(outputs, "section", 1)
        return (received, input_store, preact_store, act_partial)

    start_state = (
        jnp.zeros((row_count, feature_count), jnp.bfloat16),
        jnp.zeros((micro_count, row_count, feature_count), jnp.bfloat16),
        jnp.zeros((micro_count, row_count, feature_count), jnp.float32),
        jnp.zeros((nblocks, BLK, BLK), jnp.float32),
    )
    received_last, input_store, preact_store, act_partial = lax.fori_loop(
        0, tick_count, forward_tick, start_state
    )
    act_first, act_second = pack_pairs(act_partial)

    def backward_tick(tick_number, loop_state):
        received, grad_partial = loop_state
        micro_slot = tick_number - (sections - 1 - section_index)
        is_active = (micro_slot >= 0) & (micro_slot < micro_count)
        safe_slot = jnp.clip(micro_slot, 0, micro_count - 1)
        fresh_rows = lax.dynamic_index_in_dim(cotangent, safe_slot, 0, keepdims=False)
        upstream = jnp.where(section_index == sections - 1, fresh_rows, received)

        def backward_active(operands):
            upstream, grad_partial = operands
            inputs = lax.dynamic_index_in_dim(input_store, safe_slot, 0, keepdims=False)
            preact = lax.dynamic_index_in_dim(preact_store, safe_slot, 0, keepdims=False)
            deltas, downward = layer_backward(inputs, preact, upstream, scale_row, weight)
            return (downward, grad_partial + block_grams(deltas, nblocks))

        def backward_resting(operands):
            return (jnp.zeros_like(operands[0]), operands[1])

        downward, grad_partial = lax.cond(
            is_active, backward_active, backward_resting, (upstream, grad_partial)
        )
        received = shifted(downward, "section", -1)
        return (received, grad_partial)

    back_state = (
        jnp.zeros((row_count, feature_count), jnp.bfloat16),
        jnp.zeros((nblocks, BLK, BLK), jnp.float32),
    )
    received_first, grad_partial = lax.fori_loop(0, tick_count, backward_tick, back_state)
    grad_first, grad_second = pack_pairs(grad_partial)
    act_first, act_second, grad_first, grad_second = (
        lax.psum(act_first.astype(jnp.bfloat16), "dp").astype(jnp.float32),
        lax.psum(act_second.astype(jnp.bfloat16), "dp").astype(jnp.float32),
        lax.psum(grad_first.astype(jnp.bfloat16), "dp").astype(jnp.float32),
        lax.psum(grad_second.astype(jnp.bfloat16), "dp").astype(jnp.float32),
    )
    slab_rows = BLK // lax.axis_size("dp")
    slab_start = lax.axis_index("dp") * slab_rows
    act_roots = root_rows(unpack_pairs(act_first, act_second), row_total, slab_start, slab_rows)
    grad_roots = root_rows(unpack_pairs(grad_first, grad_second), row_total, slab_start, slab_rows)
    return (act_roots, grad_roots)


def solution(mesh):
    return jax.shard_map(
        shards,
        mesh=mesh,
        in_specs=(P(None, "dp", None), P(None, "dp", None), P("section", None), P("section", None)),
        out_specs=(P(("section", "dp"), None), P(("section", "dp"), None)),
        check_vma=False,
    )
```

profile of v0, /device:TPU:1, one launch (start us, length us, event | category | flops | bytes accessed | tf_op | source)
XLA Modules:
  0.0 753.1 jit_solution(16206677645667529857)
XLA Ops:
  13.3 184.2 %while.40 = (s32[]{:T(128)}, bf16[128,2048]{1,0:T(8,128)(2,1)S(1)}, bf16[2,128,2048]{2,1,0:T(8,128)(2,1)S(1)}, f32[2,128,2048]{2,1,0:T(8,128)}, f32[2,1024,1024]...) while((s32[]{:T(128)}, bf16[128,2048]{1,0:T(8,128)(2,1)S(1)}, ...), condition=%wide.region_4.5_spmd, body=%wide.region_0.4_spmd.sunk | while | flops 1618739328 | bytes 111168496 | solution.py:121
  13.3 13.5 %conditional.4 = (bf16[128,2048]{1,0:T(8,128)(2,1)S(1)}, bf16[2,128,2048]{2,1,0:T(8,128)(2,1)S(1)}, f32[2,128,2048]{2,1,0:T(8,128)}, f32[2,1024,1024]{2,1,0:T(8,128)}) conditional(s32[]{:T(128)} %convert_element_type.152, (bf16[2,128,2048]{2,1,0:T(8,128)(2,1)S(1)}, f32[2,128,2048]{2,1,0:T(8,128)}, f32[2,1024,1024]{2,1,0:T(8,128)}) %tuple.109, ...), branch_computations={%region_1.1_spmd, %region_2.3_spmd} | conditional | flops 1618739328 | bytes 109071048 | solution.py:106
  28.1 10.0 %collective-permute-done = bf16[128,2048]{1,0:T(8,128)(2,1)S(1)} collective-permute-done((bf16[128,2048]{1,0:T(8,128)(2,1)S(1)}, bf16[128,2048]{1,0:T(8,128)(2,1)S(1)}, u32[]{:S(2)}, u32[]{:S(2)}) %collective-permute-start) | collective-permute-done | bytes 524320 | tf_op jit(solution)/shard_map/while/body/eval_jaxpr/ppermute | solution.py:15
  38.2 13.5 %conditional.4 = (bf16[128,2048]{1,0:T(8,128)(2,1)S(1)}, bf16[2,128,2048]{2,1,0:T(8,128)(2,1)S(1)}, f32[2,128,2048]{2,1,0:T(8,128)}, f32[2,1024,1024]{2,1,0:T(8,128)}) conditional(s32[]{:T(128)} %convert_element_type.152, (bf16[2,128,2048]{2,1,0:T(8,128)(2,1)S(1)}, f32[2,128,2048]{2,1,0:T(8,128)}, f32[2,1024,1024]{2,1,0:T(8,128)}) %tuple.109, ...), branch_computations={%region_1.1_spmd, %region_2.3_spmd} | conditional | flops 1618739328 | bytes 109071048 | solution.py:106
  55.8 9.1 %collective-permute-done = bf16[128,2048]{1,0:T(8,128)(2,1)S(1)} collective-permute-done((bf16[128,2048]{1,0:T(8,128)(2,1)S(1)}, bf16[128,2048]{1,0:T(8,128)(2,1)S(1)}, u32[]{:S(2)}, u32[]{:S(2)}) %collective-permute-start) | collective-permute-done | bytes 524320 | tf_op jit(solution)/shard_map/while/body/eval_jaxpr/ppermute | solution.py:15
  65.0 17.6 %collective-permute-start = (bf16[128,2048]{1,0:T(8,128)(2,1)S(1)}, bf16[128,2048]{1,0:T(8,128)(2,1)S(1)}, u32[]{:S(2)}, u32[]{:S(2)}) collective-permute-start(bf16[128,2048]{1,0:T(8,128)(2,1)S(1)} %get-tuple-element.781), channel_id=1, source_target_pairs={{0,16},{16,32},{32,48},{48,64},{64,80},{80,96},{96,112},{1,17},{17... | collective-permute-start | bytes 1572872 | tf_op jit(solution)/shard_map/while/body/eval_jaxpr/ppermute | solution.py:15
  82.6 8.2 %collective-permute-done = bf16[128,2048]{1,0:T(8,128)(2,1)S(1)} collective-permute-done((bf16[128,2048]{1,0:T(8,128)(2,1)S(1)}, bf16[128,2048]{1,0:T(8,128)(2,1)S(1)}, u32[]{:S(2)}, u32[]{:S(2)}) %collective-permute-start) | collective-permute-done | bytes 524320 | tf_op jit(solution)/shard_map/while/body/eval_jaxpr/ppermute | solution.py:15
  95.0 7.3 collective-permute-done
  102.4 16.2 %collective-permute-start = (bf16[128,2048]{1,0:T(8,128)(2,1)S(1)}, bf16[128,2048]{1,0:T(8,128)(2,1)S(1)}, u32[]{:S(2)}, u32[]{:S(2)}) collective-permute-start(bf16[128,2048]{1,0:T(8,128)(2,1)S(1)} %get-tuple-element.781), channel_id=1, source_target_pairs={{0,16},{16,32},{32,48},{48,64},{64,80},{80,96},{96,112},{1,17},{17... | collective-permute-start | bytes 1572872 | tf_op jit(solution)/shard_map/while/body/eval_jaxpr/ppermute | solution.py:15
  118.6 6.6 collective-permute-done
  129.5 6.4 collective-permute-done
  136.0 15.8 %collective-permute-start = (bf16[128,2048]{1,0:T(8,128)(2,1)S(1)}, bf16[128,2048]{1,0:T(8,128)(2,1)S(1)}, u32[]{:S(2)}, u32[]{:S(2)}) collective-permute-start(bf16[128,2048]{1,0:T(8,128)(2,1)S(1)} %get-tuple-element.781), channel_id=1, source_target_pairs={{0,16},{16,32},{32,48},{48,64},{64,80},{80,96},{96,112},{1,17},{17... | collective-permute-start | bytes 1572872 | tf_op jit(solution)/shard_map/while/body/eval_jaxpr/ppermute | solution.py:15
  151.8 6.1 collective-permute-done
  157.9 6.2 collective-permute-start
  170.2 21.2 %collective-permute-start = (bf16[128,2048]{1,0:T(8,128)(2,1)S(1)}, bf16[128,2048]{1,0:T(8,128)(2,1)S(1)}, u32[]{:S(2)}, u32[]{:S(2)}) collective-permute-start(bf16[128,2048]{1,0:T(8,128)(2,1)S(1)} %get-tuple-element.781), channel_id=1, source_target_pairs={{0,16},{16,32},{32,48},{48,64},{64,80},{80,96},{96,112},{1,17},{17... | collective-permute-start | bytes 1572872 | tf_op jit(solution)/shard_map/while/body/eval_jaxpr/ppermute | solution.py:15
  197.5 6.1 convert_bitcast_fusion.1
  207.9 265.1 %while.41 = (s32[]{:T(128)}, bf16[128,2048]{1,0:T(8,128)(2,1)S(1)}, f32[2,1024,1024]{2,1,0:T(8,128)}, s32[]{:T(128)}, pred[]{:T(512)}, /*index=5*/bf16[2,128,204...) while((s32[]{:T(128)}, bf16[128,2048]{1,0:T(8,128)(2,1)S(1)}, ...), condition=%wide.region_14.15_spmd, body=%wide.region_9.0_spmd.sunk | while | flops 1622933632 | bytes 94909336 | solution.py:154
  209.3 13.2 %collective-permute-done.1 = bf16[128,2048]{1,0:T(8,128)(2,1)S(1)} collective-permute-done((bf16[128,2048]{1,0:T(8,128)(2,1)S(1)}, bf16[128,2048]{1,0:T(8,128)(2,1)S(1)}, u32[]{:S(2)}, u32[]{:S(2)}) %collective-permute-start.1) | collective-permute-done | bytes 524320 | tf_op jit(solution)/shard_map/while/body/eval_jaxpr/ppermute | solution.py:15
  223.9 17.3 %collective-permute-done.1 = bf16[128,2048]{1,0:T(8,128)(2,1)S(1)} collective-permute-done((bf16[128,2048]{1,0:T(8,128)(2,1)S(1)}, bf16[128,2048]{1,0:T(8,128)(2,1)S(1)}, u32[]{:S(2)}, u32[]{:S(2)}) %collective-permute-start.1) | collective-permute-done | bytes 524320 | tf_op jit(solution)/shard_map/while/body/eval_jaxpr/ppermute | solution.py:15
  242.5 16.6 %collective-permute-done.1 = bf16[128,2048]{1,0:T(8,128)(2,1)S(1)} collective-permute-done((bf16[128,2048]{1,0:T(8,128)(2,1)S(1)}, bf16[128,2048]{1,0:T(8,128)(2,1)S(1)}, u32[]{:S(2)}, u32[]{:S(2)}) %collective-permute-start.1) | collective-permute-done | bytes 524320 | tf_op jit(solution)/shard_map/while/body/eval_jaxpr/ppermute | solution.py:15
  260.5 13.0 %collective-permute-done.1 = bf16[128,2048]{1,0:T(8,128)(2,1)S(1)} collective-permute-done((bf16[128,2048]{1,0:T(8,128)(2,1)S(1)}, bf16[128,2048]{1,0:T(8,128)(2,1)S(1)}, u32[]{:S(2)}, u32[]{:S(2)}) %collective-permute-start.1) | collective-permute-done | bytes 524320 | tf_op jit(solution)/shard_map/while/body/eval_jaxpr/ppermute | solution.py:15
  274.9 27.9 %collective-permute-done.1 = bf16[128,2048]{1,0:T(8,128)(2,1)S(1)} collective-permute-done((bf16[128,2048]{1,0:T(8,128)(2,1)S(1)}, bf16[128,2048]{1,0:T(8,128)(2,1)S(1)}, u32[]{:S(2)}, u32[]{:S(2)}) %collective-permute-start.1) | collective-permute-done | bytes 524320 | tf_op jit(solution)/shard_map/while/body/eval_jaxpr/ppermute | solution.py:15
  304.2 14.4 %collective-permute-done.1 = bf16[128,2048]{1,0:T(8,128)(2,1)S(1)} collective-permute-done((bf16[128,2048]{1,0:T(8,128)(2,1)S(1)}, bf16[128,2048]{1,0:T(8,128)(2,1)S(1)}, u32[]{:S(2)}, u32[]{:S(2)}) %collective-permute-start.1) | collective-permute-done | bytes 524320 | tf_op jit(solution)/shard_map/while/body/eval_jaxpr/ppermute | solution.py:15
  320.0 99.7 %collective-permute-done.1 = bf16[128,2048]{1,0:T(8,128)(2,1)S(1)} collective-permute-done((bf16[128,2048]{1,0:T(8,128)(2,1)S(1)}, bf16[128,2048]{1,0:T(8,128)(2,1)S(1)}, u32[]{:S(2)}, u32[]{:S(2)}) %collective-permute-start.1) | collective-permute-done | bytes 524320 | tf_op jit(solution)/shard_map/while/body/eval_jaxpr/ppermute | solution.py:15
  419.7 14.9 %conditional.5 = (bf16[128,2048]{1,0:T(8,128)(2,1)S(1)}, f32[2,1024,1024]{2,1,0:T(8,128)}) conditional(s32[]{:T(128)} %convert_element_type.153, f32[2,1024,1024]{2,1,0:T(8,128)} %get-tuple-element.863, (pred[]{:T(512)}, s32[]{:T(128)}, bf16[2,128,2048]{2,1,0:T(8,128)(2,1)S(1)}, bf16[128,2048]{1,0:T(8,128)(2,1)S(1)}, ...), branch_computations={%region_10.10_spmd, %region_11.13_spmd} | conditional | flops 1622933632 | bytes 92811912 | solution.py:144
  422.1 6.5 fusion.15
  435.9 12.2 %collective-permute-done.1 = bf16[128,2048]{1,0:T(8,128)(2,1)S(1)} collective-permute-done((bf16[128,2048]{1,0:T(8,128)(2,1)S(1)}, bf16[128,2048]{1,0:T(8,128)(2,1)S(1)}, u32[]{:S(2)}, u32[]{:S(2)}) %collective-permute-start.1) | collective-permute-done | bytes 524320 | tf_op jit(solution)/shard_map/while/body/eval_jaxpr/ppermute | solution.py:15
  448.2 14.9 %conditional.5 = (bf16[128,2048]{1,0:T(8,128)(2,1)S(1)}, f32[2,1024,1024]{2,1,0:T(8,128)}) conditional(s32[]{:T(128)} %convert_element_type.153, f32[2,1024,1024]{2,1,0:T(8,128)} %get-tuple-element.863, (pred[]{:T(512)}, s32[]{:T(128)}, bf16[2,128,2048]{2,1,0:T(8,128)(2,1)S(1)}, bf16[128,2048]{1,0:T(8,128)(2,1)S(1)}, ...), branch_computations={%region_10.10_spmd, %region_11.13_spmd} | conditional | flops 1622933632 | bytes 92811912 | solution.py:144
  450.5 6.5 fusion.15
  464.4 8.6 %collective-permute-done.1 = bf16[128,2048]{1,0:T(8,128)(2,1)S(1)} collective-permute-done((bf16[128,2048]{1,0:T(8,128)(2,1)S(1)}, bf16[128,2048]{1,0:T(8,128)(2,1)S(1)}, u32[]{:S(2)}, u32[]{:S(2)}) %collective-permute-start.1) | collective-permute-done | bytes 524320 | tf_op jit(solution)/shard_map/while/body/eval_jaxpr/ppermute | solution.py:15
  486.6 210.7 %all-reduce.3.cloned.1.call-done = (bf16[1,1,1024,1024]{3,2,1,0:T(8,128)(2,1)}, bf16[1,1,1024,1024]{3,2,1,0:T(8,128)(2,1)}, bf16[1,1,1024,1024]{3,2,1,0:T(8,128)(2,1)}, bf16[1,1,1024,1024]{3,2,1,0:T(8,128)(2,1)}) async-done(((bf16[1,1,1024,1024]{3,2,1,0:T(8,128)(2,1)}, bf16[1,1,1024,1024]{3,2,1,0:T(8,128)(2,1)}, bf16[1,1,1024,1024]{3,2,1,0:T(8,128)(2,1)}, bf16[1,1,1024,1024]{3,2,1,0:T(8,128)(2,1)}), ...) | async-done | bytes 8388624 | tf_op jit(solution)/shard_map/psum | solution.py:160
  703.6 6.6 fusion.32
  (136 shorter events, 148.5 us)
Async XLA Ops:
  7.2 6.1 copy-start.7
  7.2 690.1 %all-reduce.3.cloned.1.call-start = ((), (), s32[]{:S(2)}) async-start(), calls=%async_computation | async-start | bytes 16777216 | tf_op jit(solution)/shard_map/psum | solution.py:160
  14.7 5.6 slice-start
  14.7 5.3 copy-start.4
  14.7 6.5 slice-start.1
  26.8 11.4 %collective-permute-start = (bf16[128,2048]{1,0:T(8,128)(2,1)S(1)}, bf16[128,2048]{1,0:T(8,128)(2,1)S(1)}, u32[]{:S(2)}, u32[]{:S(2)}) collective-permute-start(bf16[128,2048]{1,0:T(8,128)(2,1)S(1)} %get-tuple-element.781), channel_id=1, source_target_pairs={{0,16},{16,32},{32,48},{48,64},{64,80},{80,96},{96,112},{1,17},{17... | collective-permute-start | bytes 1572872 | tf_op jit(solution)/shard_map/while/body/eval_jaxpr/ppermute | solution.py:15
  39.6 5.6 slice-start
  39.6 5.3 copy-start.4
  39.6 6.5 slice-start.1
  51.7 13.3 %collective-permute-start = (bf16[128,2048]{1,0:T(8,128)(2,1)S(1)}, bf16[128,2048]{1,0:T(8,128)(2,1)S(1)}, u32[]{:S(2)}, u32[]{:S(2)}) collective-permute-start(bf16[128,2048]{1,0:T(8,128)(2,1)S(1)} %get-tuple-element.781), channel_id=1, source_target_pairs={{0,16},{16,32},{32,48},{48,64},{64,80},{80,96},{96,112},{1,17},{17... | collective-permute-start | bytes 1572872 | tf_op jit(solution)/shard_map/while/body/eval_jaxpr/ppermute | solution.py:15
  65.0 25.8 %collective-permute-start = (bf16[128,2048]{1,0:T(8,128)(2,1)S(1)}, bf16[128,2048]{1,0:T(8,128)(2,1)S(1)}, u32[]{:S(2)}, u32[]{:S(2)}) collective-permute-start(bf16[128,2048]{1,0:T(8,128)(2,1)S(1)} %get-tuple-element.781), channel_id=1, source_target_pairs={{0,16},{16,32},{32,48},{48,64},{64,80},{80,96},{96,112},{1,17},{17... | collective-permute-start | bytes 1572872 | tf_op jit(solution)/shard_map/while/body/eval_jaxpr/ppermute | solution.py:15
  90.9 11.4 %collective-permute-start = (bf16[128,2048]{1,0:T(8,128)(2,1)S(1)}, bf16[128,2048]{1,0:T(8,128)(2,1)S(1)}, u32[]{:S(2)}, u32[]{:S(2)}) collective-permute-start(bf16[128,2048]{1,0:T(8,128)(2,1)S(1)} %get-tuple-element.781), channel_id=1, source_target_pairs={{0,16},{16,32},{32,48},{48,64},{64,80},{80,96},{96,112},{1,17},{17... | collective-permute-start | bytes 1572872 | tf_op jit(solution)/shard_map/while/body/eval_jaxpr/ppermute | solution.py:15
  102.4 22.9 %collective-permute-start = (bf16[128,2048]{1,0:T(8,128)(2,1)S(1)}, bf16[128,2048]{1,0:T(8,128)(2,1)S(1)}, u32[]{:S(2)}, u32[]{:S(2)}) collective-permute-start(bf16[128,2048]{1,0:T(8,128)(2,1)S(1)} %get-tuple-element.781), channel_id=1, source_target_pairs={{0,16},{16,32},{32,48},{48,64},{64,80},{80,96},{96,112},{1,17},{17... | collective-permute-start | bytes 1572872 | tf_op jit(solution)/shard_map/while/body/eval_jaxpr/ppermute | solution.py:15
  125.3 10.6 %collective-permute-start = (bf16[128,2048]{1,0:T(8,128)(2,1)S(1)}, bf16[128,2048]{1,0:T(8,128)(2,1)S(1)}, u32[]{:S(2)}, u32[]{:S(2)}) collective-permute-start(bf16[128,2048]{1,0:T(8,128)(2,1)S(1)} %get-tuple-element.781), channel_id=1, source_target_pairs={{0,16},{16,32},{32,48},{48,64},{64,80},{80,96},{96,112},{1,17},{17... | collective-permute-start | bytes 1572872 | tf_op jit(solution)/shard_map/while/body/eval_jaxpr/ppermute | solution.py:15
  136.0 21.9 %collective-permute-start = (bf16[128,2048]{1,0:T(8,128)(2,1)S(1)}, bf16[128,2048]{1,0:T(8,128)(2,1)S(1)}, u32[]{:S(2)}, u32[]{:S(2)}) collective-permute-start(bf16[128,2048]{1,0:T(8,128)(2,1)S(1)} %get-tuple-element.781), channel_id=1, source_target_pairs={{0,16},{16,32},{32,48},{48,64},{64,80},{80,96},{96,112},{1,17},{17... | collective-permute-start | bytes 1572872 | tf_op jit(solution)/shard_map/while/body/eval_jaxpr/ppermute | solution.py:15
  157.9 12.2 %collective-permute-start = (bf16[128,2048]{1,0:T(8,128)(2,1)S(1)}, bf16[128,2048]{1,0:T(8,128)(2,1)S(1)}, u32[]{:S(2)}, u32[]{:S(2)}) collective-permute-start(bf16[128,2048]{1,0:T(8,128)(2,1)S(1)} %get-tuple-element.781), channel_id=1, source_target_pairs={{0,16},{16,32},{32,48},{48,64},{64,80},{80,96},{96,112},{1,17},{17... | collective-permute-start | bytes 1572872 | tf_op jit(solution)/shard_map/while/body/eval_jaxpr/ppermute | solution.py:15
  170.2 27.3 %collective-permute-start = (bf16[128,2048]{1,0:T(8,128)(2,1)S(1)}, bf16[128,2048]{1,0:T(8,128)(2,1)S(1)}, u32[]{:S(2)}, u32[]{:S(2)}) collective-permute-start(bf16[128,2048]{1,0:T(8,128)(2,1)S(1)} %get-tuple-element.781), channel_id=1, source_target_pairs={{0,16},{16,32},{32,48},{48,64},{64,80},{80,96},{96,112},{1,17},{17... | collective-permute-start | bytes 1572872 | tf_op jit(solution)/shard_map/while/body/eval_jaxpr/ppermute | solution.py:15
  197.5 10.5 %copy-start.3 = (bf16[2,128,2048]{2,1,0:T(8,128)(2,1)S(1)}, bf16[2,128,2048]{2,1,0:T(8,128)(2,1)}, u32[]{:S(2)}) copy-start(bf16[2,128,2048]{2,1,0:T(8,128)(2,1)} %param.13) | copy-start | bytes 3145732
  208.0 14.5 %collective-permute-start.1 = (bf16[128,2048]{1,0:T(8,128)(2,1)S(1)}, bf16[128,2048]{1,0:T(8,128)(2,1)S(1)}, u32[]{:S(2)}, u32[]{:S(2)}) collective-permute-start(bf16[128,2048]{1,0:T(8,128)(2,1)S(1)} %get-tuple-element.795), channel_id=1, source_target_pairs={{16,0},{32,16},{48,32},{64,48},{80,64},{96,80},{112,96},{17,1},{33... | collective-permute-start | bytes 1572872 | tf_op jit(solution)/shard_map/while/body/eval_jaxpr/ppermute | solution.py:15
  222.6 18.6 %collective-permute-start.1 = (bf16[128,2048]{1,0:T(8,128)(2,1)S(1)}, bf16[128,2048]{1,0:T(8,128)(2,1)S(1)}, u32[]{:S(2)}, u32[]{:S(2)}) collective-permute-start(bf16[128,2048]{1,0:T(8,128)(2,1)S(1)} %get-tuple-element.795), channel_id=1, source_target_pairs={{16,0},{32,16},{48,32},{64,48},{80,64},{96,80},{112,96},{17,1},{33... | collective-permute-start | bytes 1572872 | tf_op jit(solution)/shard_map/while/body/eval_jaxpr/ppermute | solution.py:15
  241.2 18.0 %collective-permute-start.1 = (bf16[128,2048]{1,0:T(8,128)(2,1)S(1)}, bf16[128,2048]{1,0:T(8,128)(2,1)S(1)}, u32[]{:S(2)}, u32[]{:S(2)}) collective-permute-start(bf16[128,2048]{1,0:T(8,128)(2,1)S(1)} %get-tuple-element.795), channel_id=1, source_target_pairs={{16,0},{32,16},{48,32},{64,48},{80,64},{96,80},{112,96},{17,1},{33... | collective-permute-start | bytes 1572872 | tf_op jit(solution)/shard_map/while/body/eval_jaxpr/ppermute | solution.py:15
  259.2 14.3 %collective-permute-start.1 = (bf16[128,2048]{1,0:T(8,128)(2,1)S(1)}, bf16[128,2048]{1,0:T(8,128)(2,1)S(1)}, u32[]{:S(2)}, u32[]{:S(2)}) collective-permute-start(bf16[128,2048]{1,0:T(8,128)(2,1)S(1)} %get-tuple-element.795), channel_id=1, source_target_pairs={{16,0},{32,16},{48,32},{64,48},{80,64},{96,80},{112,96},{17,1},{33... | collective-permute-start | bytes 1572872 | tf_op jit(solution)/shard_map/while/body/eval_jaxpr/ppermute | solution.py:15
  273.6 29.2 %collective-permute-start.1 = (bf16[128,2048]{1,0:T(8,128)(2,1)S(1)}, bf16[128,2048]{1,0:T(8,128)(2,1)S(1)}, u32[]{:S(2)}, u32[]{:S(2)}) collective-permute-start(bf16[128,2048]{1,0:T(8,128)(2,1)S(1)} %get-tuple-element.795), channel_id=1, source_target_pairs={{16,0},{32,16},{48,32},{64,48},{80,64},{96,80},{112,96},{17,1},{33... | collective-permute-start | bytes 1572872 | tf_op jit(solution)/shard_map/while/body/eval_jaxpr/ppermute | solution.py:15
  302.9 15.7 %collective-permute-start.1 = (bf16[128,2048]{1,0:T(8,128)(2,1)S(1)}, bf16[128,2048]{1,0:T(8,128)(2,1)S(1)}, u32[]{:S(2)}, u32[]{:S(2)}) collective-permute-start(bf16[128,2048]{1,0:T(8,128)(2,1)S(1)} %get-tuple-element.795), channel_id=1, source_target_pairs={{16,0},{32,16},{48,32},{64,48},{80,64},{96,80},{112,96},{17,1},{33... | collective-permute-start | bytes 1572872 | tf_op jit(solution)/shard_map/while/body/eval_jaxpr/ppermute | solution.py:15
  318.7 101.0 %collective-permute-start.1 = (bf16[128,2048]{1,0:T(8,128)(2,1)S(1)}, bf16[128,2048]{1,0:T(8,128)(2,1)S(1)}, u32[]{:S(2)}, u32[]{:S(2)}) collective-permute-start(bf16[128,2048]{1,0:T(8,128)(2,1)S(1)} %get-tuple-element.795), channel_id=1, source_target_pairs={{16,0},{32,16},{48,32},{64,48},{80,64},{96,80},{112,96},{17,1},{33... | collective-permute-start | bytes 1572872 | tf_op jit(solution)/shard_map/while/body/eval_jaxpr/ppermute | solution.py:15
  419.7 9.3 %slice-start.2 = ((s8[8388608]{0:T(1024)(128)(4,1)}), s8[4194304]{0:T(1024)(128)(4,1)S(1)}, s32[]{:S(2)}) async-start(s8[8388608]{0:T(1024)(128)(4,1)} %bitcast.69), calls=%async_computation.3 | async-start | bytes 8388608 | tf_op jit(solution)/shard_map/while/body/eval_jaxpr/cond
  422.1 7.0 slice-start.3
  434.6 13.5 %collective-permute-start.1 = (bf16[128,2048]{1,0:T(8,128)(2,1)S(1)}, bf16[128,2048]{1,0:T(8,128)(2,1)S(1)}, u32[]{:S(2)}, u32[]{:S(2)}) collective-permute-start(bf16[128,2048]{1,0:T(8,128)(2,1)S(1)} %get-tuple-element.795), channel_id=1, source_target_pairs={{16,0},{32,16},{48,32},{64,48},{80,64},{96,80},{112,96},{17,1},{33... | collective-permute-start | bytes 1572872 | tf_op jit(solution)/shard_map/while/body/eval_jaxpr/ppermute | solution.py:15
  448.2 9.3 %slice-start.2 = ((s8[8388608]{0:T(1024)(128)(4,1)}), s8[4194304]{0:T(1024)(128)(4,1)S(1)}, s32[]{:S(2)}) async-start(s8[8388608]{0:T(1024)(128)(4,1)} %bitcast.69), calls=%async_computation.3 | async-start | bytes 8388608 | tf_op jit(solution)/shard_map/while/body/eval_jaxpr/cond
  450.5 7.0 slice-start.3
  463.1 9.9 %collective-permute-start.1 = (bf16[128,2048]{1,0:T(8,128)(2,1)S(1)}, bf16[128,2048]{1,0:T(8,128)(2,1)S(1)}, u32[]{:S(2)}, u32[]{:S(2)}) collective-permute-start(bf16[128,2048]{1,0:T(8,128)(2,1)S(1)} %get-tuple-element.795), channel_id=1, source_target_pairs={{16,0},{32,16},{48,32},{64,48},{80,64},{96,80},{112,96},{17,1},{33... | collective-permute-start | bytes 1572872 | tf_op jit(solution)/shard_map/while/body/eval_jaxpr/ppermute | solution.py:15
  703.6 6.6 copy-start.2
  (7 other events, 24.4 us)
Sparse Core Ops, SparseCore 0:
  481.4 215.8 all-reduce.2
where the time goes:
time: 764 us; the launch traced here: 753 us
  waiting for transfers between devices  500 us (65%)
  starting transfers between devices  102 us (13%)
  matrix products  67 us (9%)
  other arithmetic  37.3 us (5%)
  local copies, waits for them, and re-layouts  31.6 us (4%)
  between operations  14.4 us (2%)
    ppermute x18, waiting for transfers between devices, shifted(): lax.ppermute(value, axis, [(source, source + steps) for source in range(l...  289 us
    psum x1, waiting for transfers between devices, shards(): lax.psum(grad_second.astype(jnp.bfloat16), 'dp').astype(jnp.float32)  211 us
    ppermute x18, starting transfers between devices, shifted(): lax.ppermute(value, axis, [(source, source + steps) for source in range(l...  102 us
  transfers between devices with their start and end apart: 19, of which 19 were waited for; matrix products, arithmetic and copies ran while one was open for 1% of the time, Pallas kernels for 0%

commit v1 on v0

v1 whole, which is shorter than its diff:
```python
import functools

import jax
import jax.numpy as jnp
from jax import lax
from jax.experimental import pallas as pl
from jax.experimental.pallas import tpu as pltpu
from jax.sharding import PartitionSpec as P

MESH = pl.DeviceIdType.MESH
F32 = jnp.float32
BF16 = jnp.bfloat16

D = 2048
BLK = 1024
ROWS = 256
R = 32
M = ROWS // R
TN = 256
NT = D // TN
CHIPS = 8
SLAB = BLK // CHIPS
HALF = SLAB // 2
KEPT = 5
ROW_TOTAL = 4096.0
DAMPING = 4.0
SECTIONS = 8
LAG = 3

GELU_A = 0.7978845608028654
GELU_B = 0.044715


def gelu_value(z):
    t = jnp.tanh(GELU_A * (z + GELU_B * (z * z * z)))
    return 0.5 * z * (1.0 + t)


def gelu_slope(z):
    sq = z * z
    t = jnp.tanh(GELU_A * (z + GELU_B * (sq * z)))
    return 0.5 * (1.0 + t) + 0.5 * z * (1.0 - t * t) * (GELU_A * (1.0 + 3.0 * GELU_B * sq))


def kernel(
    tok, cot, gain, wgt, act_out, grad_out,
    w, wt, xs, ys, sendf, sendb, zs, ns, ds, rinvs, sib, gram, rs, ag, full, slab, ztile,
    w_sem, tok_sem, f_send, f_recv, b_send, b_recv, sib_send, sib_recv,
    rs_send, rs_recv, ag_send, ag_recv, own_sem, out_send, out_recv,
):
    s = lax.axis_index("section")
    d = lax.axis_index("dp")
    chip = d // 2
    core = d % 2
    nxt = (jnp.minimum(s + 1, SECTIONS - 1), d)
    prv = (jnp.maximum(s - 1, 0), d)
    sibling = (s, chip * 2 + 1 - core)
    first = s == 0
    last = s == SECTIONS - 1

    def peer(k):
        return (s, k * 2 + core)

    def w_copy(j):
        cols = pl.ds(j * TN, TN)
        return pltpu.make_async_copy(wgt.at[:, cols], w.at[:, cols], w_sem.at[j])

    for j in range(NT):
        w_copy(j).start()

    def rows_copy(source, target, j):
        half = ROWS // 2
        return [
            pltpu.make_async_copy(
                source.at[mb, :, pl.ds(j * TN, TN)], target.at[j, pl.ds(mb * half, half), :], tok_sem.at[j * 2 + mb]
            )
            for mb in range(2)
        ]

    @pl.when(first)
    def _():
        for j in range(NT):
            for cp in rows_copy(tok, xs, j):
                cp.start()

    @pl.when(last)
    def _():
        for j in range(NT):
            for cp in rows_copy(cot, ys, j):
                cp.start()

    barrier = pltpu.get_barrier_semaphore()
    for k in range(1, CHIPS):
        pl.semaphore_signal(barrier, inc=1, device_id=peer((chip + k) % CHIPS), device_id_type=MESH)
    pl.semaphore_signal(barrier, inc=1, device_id=sibling, device_id_type=MESH)

    @pl.when(s < SECTIONS - 1)
    def _():
        pl.semaphore_signal(barrier, inc=1, device_id=nxt, device_id_type=MESH)

    @pl.when(s > 0)
    def _():
        pl.semaphore_signal(barrier, inc=1, device_id=prv, device_id_type=MESH)

    pl.semaphore_wait(barrier, CHIPS + jnp.where(first, 0, 1) + jnp.where(last, 0, 1))

    @pl.when(first)
    def _():
        for j in range(NT):
            for cp in rows_copy(tok, xs, j):
                cp.wait()

    @pl.when(last)
    def _():
        for j in range(NT):
            for cp in rows_copy(cot, ys, j):
                cp.wait()

    for j in range(NT):
        w_copy(j).wait()

    def transpose_weight():
        def body(k, _):
            kr = pl.ds(pl.multiple_of(k * TN, TN), TN)
            for j in range(NT):
                wt[j * TN : (j + 1) * TN, kr] = w[kr, j * TN : (j + 1) * TN].T
            return 0

        lax.fori_loop(0, NT, body, 0)

    def chunk_rows(m):
        return pl.ds(pl.multiple_of(m * R, R), R)

    def f_copy(m, part):
        rows = chunk_rows(m)
        return pltpu.make_async_remote_copy(
            src_ref=sendf.at[part, rows, :], dst_ref=xs.at[part, rows, :],
            send_sem=f_send.at[m], recv_sem=f_recv.at[m], device_id=nxt, device_id_type=MESH,
        )

    def b_copy(m, part):
        rows = chunk_rows(m)
        return pltpu.make_async_remote_copy(
            src_ref=sendb.at[part, rows, :], dst_ref=ys.at[part, rows, :],
            send_sem=b_send.at[m], recv_sem=b_recv.at[m], device_id=prv, device_id_type=MESH,
        )

    whole = pl.ds(0, NT)

    def sib_copy(f, m):
        rows = chunk_rows(m)
        store = ns if f == 0 else ds
        return pltpu.make_async_remote_copy(
            src_ref=store.at[rows, pl.ds(pl.multiple_of((1 - core) * BLK, BLK), BLK)], dst_ref=sib.at[f, rows, :],
            send_sem=sib_send.at[f, m], recv_sem=sib_recv.at[f, m], device_id=sibling, device_id_type=MESH,
        )

    def forward(m, send):
        rows = chunk_rows(m)
        total = jnp.zeros((R, TN), F32)
        for j in range(NT):
            xj = xs[j, rows, :].astype(F32)
            total = total + xj * xj
        rinv = lax.rsqrt(jnp.sum(total, axis=-1, keepdims=True) * (1.0 / D) + 1e-06)
        rinvs[rows, :] = jnp.broadcast_to(rinv, (R, 128))
        for j in range(NT):
            cols = slice(j * TN, (j + 1) * TN)
            ns[rows, cols] = (xs[j, rows, :].astype(F32) * rinv * gain[:, cols]).astype(BF16)
        normed = ns[rows, :]
        for j in range(NT):
            cols = slice(j * TN, (j + 1) * TN)
            z = jnp.dot(normed, w[:, cols], preferred_element_type=F32)
            zs[rows, cols] = z
            if send:
                sendf[j, rows, :] = (xs[j, rows, :].astype(F32) + gelu_value(z)).astype(BF16)
                f_copy(m, j).start()
        sib_copy(0, m).start()

    def backward(m, send):
        rows = chunk_rows(m)
        total = jnp.zeros((R, TN), F32)
        for j in range(NT):
            cols = slice(j * TN, (j + 1) * TN)
            z = zs[rows, cols]
            delta = (ys[j, rows, :].astype(F32) * gelu_slope(z)).astype(BF16)
            ds[rows, cols] = delta
            total = total + delta.astype(F32) * z
        if send:
            rinv = rinvs[rows, :1]
            pull = jnp.sum(total, axis=-1, keepdims=True) * (1.0 / D) * rinv
            deltas = ds[rows, :]
            for j in range(NT):
                cols = slice(j * TN, (j + 1) * TN)
                dn = jnp.dot(deltas, wt[:, cols], preferred_element_type=F32)
                xj = xs[j, rows, :].astype(F32)
                dy = ys[j, rows, :].astype(F32) + rinv * (dn * gain[:, cols] - xj * pull)
                sendb[j, rows, :] = dy.astype(BF16)
                b_copy(m, j).start()
        sib_copy(1, m).start()

    def forward_step(m):
        @pl.when(s > 0)
        def _():
            f_copy(m, whole).wait_recv()

        @pl.when(s < SECTIONS - 1)
        def _():
            forward(m, True)

        @pl.when(last)
        def _():
            forward(m, False)

    def backward_step(m):
        @pl.when(s < SECTIONS - 1)
        def _():
            b_copy(m, whole).wait_recv()

        @pl.when(s > 0)
        def _():
            backward(m, True)

        @pl.when(first)
        def _():
            backward(m, False)

    def rs_copy(f, k):
        return pltpu.make_async_remote_copy(
            src_ref=gram.at[f, pl.ds(k, KEPT), pl.ds(pl.multiple_of(k * SLAB, SLAB), SLAB), :],
            dst_ref=rs.at[f, chip],
            send_sem=rs_send.at[f, k], recv_sem=rs_recv.at[f, chip], device_id=peer(k), device_id_type=MESH,
        )

    def rs_arrival(f, k):
        return pltpu.make_async_remote_copy(
            src_ref=rs.at[f, k], dst_ref=rs.at[f, k],
            send_sem=rs_send.at[f, k], recv_sem=rs_recv.at[f, k], device_id=peer(k), device_id_type=MESH,
        )

    def ag_copy(f, k):
        return pltpu.make_async_remote_copy(
            src_ref=ag.at[f, chip], dst_ref=ag.at[f, chip],
            send_sem=ag_send.at[f, k], recv_sem=ag_recv.at[f, chip], device_id=peer(k), device_id_type=MESH,
        )

    def ag_arrival(f, k):
        return pltpu.make_async_remote_copy(
            src_ref=ag.at[f, k], dst_ref=ag.at[f, k],
            send_sem=ag_send.at[f, k], recv_sem=ag_recv.at[f, k], device_id=peer(k), device_id_type=MESH,
        )

    def each_peer(fn):
        def body(k, _):
            fn((chip + k) % CHIPS)
            return 0

        lax.fori_loop(1, CHIPS, body, 0)

    def gram_send(f):
        def landed(m, _):
            sib_copy(f, m).wait_recv()
            return 0

        lax.fori_loop(0, M, landed, 0)
        store = ns if f == 0 else ds
        mine = pl.ds(pl.multiple_of(core * BLK, BLK), BLK)
        own = store[:, mine]
        other = sib[f]
        dims = (((0,), (0,)), ((), ()))
        for q in range(BLK // 256):
            cut = slice(q * 256, (q + 1) * 256)
            own_cut = store[:, pl.ds(pl.multiple_of(core * BLK + q * 256, 256), 256)]
            part = lax.dot_general(own_cut, own, dims, preferred_element_type=F32)
            part = part + lax.dot_general(sib[f, :, cut], other, dims, preferred_element_type=F32)
            part = part.astype(BF16)
            for t in range(CHIPS):
                tile = part[:, t * SLAB : (t + 1) * SLAB]
                gram[f, t, cut, :] = tile
                if t < KEPT - 1:
                    gram[f, t + CHIPS, cut, :] = tile
        each_peer(lambda k: rs_copy(f, k).start())

    def sum_gather(f):
        mine = pl.ds(pl.multiple_of(chip * SLAB, SLAB), SLAB)
        rs[f, chip] = gram[f, pl.ds(chip, KEPT), mine, :]
        each_peer(lambda k: rs_arrival(f, k).wait_recv())
        ri = lax.broadcasted_iota(jnp.int32, (SLAB, SLAB), 0)
        ci = lax.broadcasted_iota(jnp.int32, (SLAB, SLAB), 1)
        eye = ri == ci
        for j in range(KEPT):
            total = rs[f, 0, j].astype(F32)
            for k in range(1, CHIPS):
                total = total + rs[f, k, j].astype(F32)
            total = total * (1.0 / ROW_TOTAL)
            if j == 0:
                diag = jnp.sum(jnp.where(eye, total, 0.0), axis=0, keepdims=True) + DAMPING
                high = diag.astype(BF16).astype(F32)
                row = lax.broadcasted_iota(jnp.int32, (16, SLAB), 0)
                extra = jnp.where(row == 0, high, jnp.where(row == 1, diag - high, 0.0))
                ag[f, chip, KEPT * SLAB : KEPT * SLAB + 16, :] = extra.astype(BF16)
                total = jnp.where(eye, 0.0, total)
            ag[f, chip, j * SLAB : (j + 1) * SLAB, :] = total.astype(BF16)
        each_peer(lambda k: ag_copy(f, k).start())

    def roots(f, out):
        each_peer(lambda k: ag_arrival(f, k).wait_recv())
        pieces = []
        for k in range(CHIPS):
            here = slice(k * SLAB, (k + 1) * SLAB)
            for j in range(KEPT):
                there = (k + j) % CHIPS
                there = slice(there * SLAB, (there + 1) * SLAB)
                tile = ag[f, k, j * SLAB : (j + 1) * SLAB, :]
                full[here, there] = tile
                if 0 < j < KEPT - 1:
                    full[there, here] = tile.T
            extra = ag[f, k, KEPT * SLAB : KEPT * SLAB + 16, :].astype(F32)
            pieces.append(jnp.sum(extra, axis=0, keepdims=True))
        diag = jnp.concatenate(pieces, axis=1)
        bound = jnp.abs(diag)
        for k in range(CHIPS):
            part = jnp.abs(full[k * SLAB : (k + 1) * SLAB, :].astype(F32))
            bound = bound + jnp.sum(part, axis=0, keepdims=True)
        scale = 1.0 / jnp.max(bound, axis=1, keepdims=True)
        mine = pl.ds(pl.multiple_of(chip * SLAB, SLAB), SLAB)
        ri = lax.broadcasted_iota(jnp.int32, (SLAB, BLK), 0)
        ci = lax.broadcasted_iota(jnp.int32, (SLAB, BLK), 1)
        eye = ci == ri + chip * SLAB
        scaled_diag = diag * scale
        off = full[mine, :].astype(F32) * scale
        slab[0] = off
        slab[1] = jnp.where(eye, scaled_diag, off)

        def times(u):
            u_diag = jnp.sum(jnp.where(eye, u, 0.0), axis=1, keepdims=True)
            u_off = jnp.where(eye, 0.0, u).astype(BF16)
            prod = jnp.dot(u_off, full[...], preferred_element_type=F32) * scale
            return prod + u_diag * slab[0] + u * scaled_diag

        u = times(0.0625 * slab[1]) - 0.5625 * slab[1]
        u = times(u) + 1.6875 * slab[1]
        u = times(u) - 2.4375 * slab[1]
        ztile[f] = u + jnp.where(eye, 2.25, 0.0)
        cols = pl.ds(pl.multiple_of(core * BLK, BLK), BLK)
        to_sibling(f, out).start()
        to_out(f, out).start()

    def to_sibling(f, out):
        cols = pl.ds(pl.multiple_of(core * BLK, BLK), BLK)
        return pltpu.make_async_remote_copy(
            src_ref=ztile.at[f, pl.ds(pl.multiple_of((1 - core) * HALF, HALF), HALF), :], dst_ref=out.at[:, cols],
            send_sem=out_send.at[f], recv_sem=out_recv.at[f], device_id=sibling, device_id_type=MESH,
        )

    def to_out(f, out):
        cols = pl.ds(pl.multiple_of(core * BLK, BLK), BLK)
        return pltpu.make_async_copy(
            ztile.at[f, pl.ds(pl.multiple_of(core * HALF, HALF), HALF), :], out.at[:, cols], own_sem.at[f]
        )

    @pl.when(s >= 4)
    def _():
        transpose_weight()

    lag = jnp.minimum(M, (SECTIONS - 1 - s) * LAG)

    def first_half(i, _):
        forward_step(i)

        @pl.when(i >= lag)
        def _():
            backward_step(i - lag)

        return 0

    lax.fori_loop(0, M, first_half, 0)

    @pl.when((s >= 1) & (s < 4))
    def _():
        transpose_weight()

    @pl.when(s <= 4)
    def _():
        gram_send(0)

    @pl.when(s <= 1)
    def _():
        sum_gather(0)
        roots(0, act_out)

    def second_half(i, _):
        backward_step(i)
        return 0

    lax.fori_loop(M - lag, M, second_half, 0)

    @pl.when(s >= 5)
    def _():
        gram_send(0)

    gram_send(1)

    @pl.when(s >= 2)
    def _():
        sum_gather(0)

    sum_gather(1)

    @pl.when(s >= 2)
    def _():
        roots(0, act_out)

    roots(1, grad_out)

    for f, out in ((0, act_out), (1, grad_out)):
        to_out(f, out).wait()
        to_sibling(f, out).wait()

    def sent(m, _):
        @pl.when(s < SECTIONS - 1)
        def _():
            f_copy(m, whole).wait_send()

        @pl.when(s > 0)
        def _():
            b_copy(m, whole).wait_send()

        sib_copy(0, m).wait_send()
        sib_copy(1, m).wait_send()
        return 0

    lax.fori_loop(0, M, sent, 0)
    for f in range(2):
        each_peer(lambda k: rs_copy(f, k).wait_send())
        each_peer(lambda k: ag_copy(f, k).wait_send())


def shards(tokens, cotangent, gain, weight):
    out = jax.ShapeDtypeStruct((HALF, D), F32)
    dma = pltpu.SemaphoreType.DMA
    anywhere = pl.BlockSpec(memory_space=pl.ANY)
    return pl.pallas_call(
        kernel,
        out_shape=(out, out),
        in_specs=[anywhere, anywhere, pl.BlockSpec(memory_space=pltpu.VMEM), anywhere],
        out_specs=(anywhere, anywhere),
        scratch_shapes=[
            pltpu.VMEM((D, D), BF16),
            pltpu.VMEM((D, D), BF16),
            pltpu.VMEM((NT, ROWS, TN), BF16),
            pltpu.VMEM((NT, ROWS, TN), BF16),
            pltpu.VMEM((NT, ROWS, TN), BF16),
            pltpu.VMEM((NT, ROWS, TN), BF16),
            pltpu.VMEM((ROWS, D), F32),
            pltpu.VMEM((ROWS, D), BF16),
            pltpu.VMEM((ROWS, D), BF16),
            pltpu.VMEM((ROWS, 128), F32),
            pltpu.VMEM((2, ROWS, BLK), BF16),
            pltpu.VMEM((2, CHIPS + KEPT - 1, BLK, SLAB), BF16),
            pltpu.VMEM((2, CHIPS, KEPT, SLAB, SLAB), BF16),
            pltpu.VMEM((2, CHIPS, KEPT * SLAB + 16, SLAB), BF16),
            pltpu.VMEM((BLK, BLK), BF16),
            pltpu.VMEM((2, SLAB, BLK), F32),
            pltpu.VMEM((2, SLAB, BLK), F32),
            dma((NT,)),
            dma((2 * NT,)),
            dma((M,)),
            dma((M,)),
            dma((M,)),
            dma((M,)),
            dma((2, M)),
            dma((2, M)),
            dma((2, CHIPS)),
            dma((2, CHIPS)),
            dma((2, CHIPS)),
            dma((2, CHIPS)),
            dma((2,)),
            dma((2,)),
            dma((2,)),
        ],
        name="refresh",
        compiler_params=pltpu.CompilerParams(
            collective_id=0, has_side_effects=True, vmem_limit_bytes=58 * 2**20
        ),
    )(tokens, cotangent, gain, weight)


def solution(mesh):
    return jax.shard_map(
        shards,
        mesh=mesh,
        in_specs=(P(None, "dp", None), P(None, "dp", None), P("section", None), P("section", None)),
        out_specs=(P(("section", "dp"), None), P(("section", "dp"), None)),
        check_vma=False,
    )
```

time: 764 us -> 183 us (0.24); the launches traced: 753 us -> 182 us
  waiting for transfers between devices: 500 us -> 0 us
  Pallas kernels: 0 us -> 177 us
  starting transfers between devices: 102 us -> 0 us
  matrix products: 67 us -> 0 us
  other arithmetic: 37.3 us -> 0 us
  local copies, waits for them, and re-layouts: 31.6 us -> 3.74 us
  between operations: 14.4 us -> 0.64 us
    ppermute x18 -> x0, waiting for transfers between devices: 289 us -> none  [shifted(): lax.ppermute(value, axis, [(source, source + steps) for source in range(l...]
    psum x1 -> x0, waiting for transfers between devices: 211 us -> none  [shards(): lax.psum(grad_second.astype(jnp.bfloat16), 'dp').astype(jnp.float32)]
    pallas_call x0 -> x1, Pallas kernels: none -> 177 us  [shards(): pl.pallas_call(kernel, out_shape=(out, out), in_specs=[anywhere, anywhere...]
    ppermute x18 -> x0, starting transfers between devices: 102 us -> none  [shifted(): lax.ppermute(value, axis, [(source, source + steps) for source in range(l...]
    dot_general x14 -> x0, matrix products: 67 us -> none  [the longest x2 13 us: layer_backward(): lax.dot_general(deltas, matrix, (((1,), (1,)), ((), ())), preferred_eleme...]
    cond x32 -> x0, local copies, waits for them, and re-layouts: 14.7 us -> none
    reduce_sum x5 -> x0, other arithmetic: 11.1 us -> none  [the longest x1 6.04 us: root_rows(): row_bound = jnp.max(jnp.sum(jnp.abs(damped), axis=2), axis=1)[:, None, None]]
    another operation x2 -> x0, other arithmetic: 10.3 us -> none
  transfers between devices with their start and end apart: 19 -> 0, of which waited for: 19 -> 0; matrix products, arithmetic and copies ran while one was open for 1% -> 0% of each run, Pallas kernels for 0% -> 0%
where the time goes in v1:
time: 183 us; the launch traced here: 182 us
  Pallas kernels  177 us (97%)
  local copies, waits for them, and re-layouts  3.74 us (2%)
    pallas_call x1, Pallas kernels, shards(): pl.pallas_call(kernel, out_shape=(out, out), in_specs=[anywhere, anywhere...  177 us
    unnamed x2, local copies, waits for them, and re-layouts  3.74 us

profile of v1, /device:TPU:1, one launch (start us, length us, event | category | flops | bytes accessed | tf_op | source)
XLA Modules:
  0.0 181.7 jit_solution(8298358199905817969)
XLA Ops:
  0.6 177.3 %refresh.1 = (f32[64,2048]{1,0:T(8,128)}, f32[64,2048]{1,0:T(8,128)}) custom-call(bf16[2,128,2048]{2,1,0:T(8,128)(2,1)} %tok.1, bf16[2,128,2048]{2,1,0:T(8,128)(2,1)} %cot.1, f32[1,2048]{1,0:T(1,128)} %gain.1, bf16[2048,2048]{1,0:T(8,128)(2,1)} %wgt.1), custom_call_target="tpu_custom_call" | custom-call | tf_op jit(solution)/shard_map/refresh/pallas_call | solution.py:442
  177.9 1.9 %copy.8 = f32[64,2048]{1,0:T(8,128)} copy(f32[64,2048]{1,0:T(8,128)} %get-tuple-element.4) | data formatting | bytes 1048576
  179.8 1.9 %copy.9 = f32[64,2048]{1,0:T(8,128)} copy(f32[64,2048]{1,0:T(8,128)} %get-tuple-element.5) | data formatting | bytes 1048576

commit v2 on v1

--- a/solution.py
+++ b/solution.py
@@ -26,6 +26,8 @@
 DAMPING = 4.0
 SECTIONS = 8
 LAG = 3
+PAD = 128
+EACH = 4
 
 GELU_A = 0.7978845608028654
 GELU_B = 0.044715
@@ -44,7 +46,7 @@
 
 def kernel(
     tok, cot, gain, wgt, act_out, grad_out,
-    w, wt, xs, ys, sendf, sendb, zs, ns, ds, rinvs, sib, gram, rs, ag, full, slab, ztile,
+    w, wt, xs, ys, sendf, sendb, zs, ns, ds, rinvs, sib, gram, rs, ag, full, slab, ztile, lhs,
     w_sem, tok_sem, f_send, f_recv, b_send, b_recv, sib_send, sib_recv,
     rs_send, rs_recv, ag_send, ag_recv, own_sem, out_send, out_recv,
 ):
@@ -65,29 +67,43 @@
         cols = pl.ds(j * TN, TN)
         return pltpu.make_async_copy(wgt.at[:, cols], w.at[:, cols], w_sem.at[j])
 
+    def first_load(source, target, j):
+        cols = pl.ds(j * TN, TN)
+        return pltpu.make_async_copy(source.at[0, :, cols], target.at[0, j], tok_sem.at[0])
+
+    def rest_load(source, target, j):
+        cols = pl.ds(j * TN, TN)
+        return pltpu.make_async_copy(source.at[1:M, :, cols], target.at[1:M, j], tok_sem.at[1])
+
+    def loaded(target, m):
+        @pl.when(m == 0)
+        def _():
+            pltpu.make_async_copy(target.at[0], target.at[0], tok_sem.at[0]).wait()
+
+        @pl.when(m == 1)
+        def _():
+            pltpu.make_async_copy(target.at[1:M], target.at[1:M], tok_sem.at[1]).wait()
+
+    @pl.when(first)
+    def _():
+        for j in range(NT):
+            first_load(tok, xs, j).start()
+
     for j in range(NT):
         w_copy(j).start()
 
-    def rows_copy(source, target, j):
-        half = ROWS // 2
-        return [
-            pltpu.make_async_copy(
-                source.at[mb, :, pl.ds(j * TN, TN)], target.at[j, pl.ds(mb * half, half), :], tok_sem.at[j * 2 + mb]
-            )
-            for mb in range(2)
-        ]
-
     @pl.when(first)
     def _():
         for j in range(NT):
-            for cp in rows_copy(tok, xs, j):
-                cp.start()
+            rest_load(tok, xs, j).start()
 
     @pl.when(last)
     def _():
         for j in range(NT):
-            for cp in rows_copy(cot, ys, j):
-                cp.start()
+            first_load(cot, ys, j).start()
+            rest_load(cot, ys, j).start()
+
+    lhs[...] = jnp.zeros_like(lhs)
 
     barrier = pltpu.get_barrier_semaphore()
     for k in range(1, CHIPS):
@@ -104,20 +120,10 @@
 
     pl.semaphore_wait(barrier, CHIPS + jnp.where(first, 0, 1) + jnp.where(last, 0, 1))
 
-    @pl.when(first)
-    def _():
-        for j in range(NT):
-            for cp in rows_copy(tok, xs, j):
-                cp.wait()
-
-    @pl.when(last)
-    def _():
-        for j in range(NT):
-            for cp in rows_copy(cot, ys, j):
-                cp.wait()
-
-    for j in range(NT):
-        w_copy(j).wait()
+    @pl.when(s > 0)
+    def _():
+        for j in range(NT):
+            w_copy(j).wait()
 
     def transpose_weight():
         def body(k, _):
@@ -132,16 +138,14 @@
         return pl.ds(pl.multiple_of(m * R, R), R)
 
     def f_copy(m, part):
-        rows = chunk_rows(m)
-        return pltpu.make_async_remote_copy(
-            src_ref=sendf.at[part, rows, :], dst_ref=xs.at[part, rows, :],
+        return pltpu.make_async_remote_copy(
+            src_ref=sendf.at[m, part], dst_ref=xs.at[m, part],
             send_sem=f_send.at[m], recv_sem=f_recv.at[m], device_id=nxt, device_id_type=MESH,
         )
 
     def b_copy(m, part):
-        rows = chunk_rows(m)
-        return pltpu.make_async_remote_copy(
-            src_ref=sendb.at[part, rows, :], dst_ref=ys.at[part, rows, :],
+        return pltpu.make_async_remote_copy(
+            src_ref=sendb.at[m, part], dst_ref=ys.at[m, part],
             send_sem=b_send.at[m], recv_sem=b_recv.at[m], device_id=prv, device_id_type=MESH,
         )
 
@@ -155,25 +159,30 @@
             send_sem=sib_send.at[f, m], recv_sem=sib_recv.at[f, m], device_id=sibling, device_id_type=MESH,
         )
 
-    def forward(m, send):
+    def forward(m, send, fresh=False):
         rows = chunk_rows(m)
         total = jnp.zeros((R, TN), F32)
         for j in range(NT):
-            xj = xs[j, rows, :].astype(F32)
+            xj = xs[m, j].astype(F32)
             total = total + xj * xj
         rinv = lax.rsqrt(jnp.sum(total, axis=-1, keepdims=True) * (1.0 / D) + 1e-06)
         rinvs[rows, :] = jnp.broadcast_to(rinv, (R, 128))
         for j in range(NT):
             cols = slice(j * TN, (j + 1) * TN)
-            ns[rows, cols] = (xs[j, rows, :].astype(F32) * rinv * gain[:, cols]).astype(BF16)
-        normed = ns[rows, :]
+            normed = (xs[m, j].astype(F32) * rinv * gain[:, cols]).astype(BF16)
+            ns[rows, cols] = normed
+            lhs[0, :R, cols] = normed
+        padded = lhs[0]
         for j in range(NT):
             cols = slice(j * TN, (j + 1) * TN)
-            z = jnp.dot(normed, w[:, cols], preferred_element_type=F32)
+            if fresh:
+                w_copy(j).wait()
+            z = jnp.dot(padded, w[:, cols], preferred_element_type=F32)[:R]
             zs[rows, cols] = z
             if send:
-                sendf[j, rows, :] = (xs[j, rows, :].astype(F32) + gelu_value(z)).astype(BF16)
-                f_copy(m, j).start()
+                sendf[m, j] = (xs[m, j].astype(F32) + gelu_value(z)).astype(BF16)
+                if (j + 1) % EACH == 0:
+                    f_copy(m, pl.ds(j + 1 - EACH, EACH)).start()
         sib_copy(0, m).start()
 
     def backward(m, send):
@@ -182,20 +191,22 @@
         for j in range(NT):
             cols = slice(j * TN, (j + 1) * TN)
             z = zs[rows, cols]
-            delta = (ys[j, rows, :].astype(F32) * gelu_slope(z)).astype(BF16)
+            delta = (ys[m, j].astype(F32) * gelu_slope(z)).astype(BF16)
             ds[rows, cols] = delta
+            lhs[1, :R, cols] = delta
             total = total + delta.astype(F32) * z
         if send:
             rinv = rinvs[rows, :1]
             pull = jnp.sum(total, axis=-1, keepdims=True) * (1.0 / D) * rinv
-            deltas = ds[rows, :]
+            padded = lhs[1]
             for j in range(NT):
                 cols = slice(j * TN, (j + 1) * TN)
-                dn = jnp.dot(deltas, wt[:, cols], preferred_element_type=F32)
-                xj = xs[j, rows, :].astype(F32)
-                dy = ys[j, rows, :].astype(F32) + rinv * (dn * gain[:, cols] - xj * pull)
-                sendb[j, rows, :] = dy.astype(BF16)
-                b_copy(m, j).start()
+                dn = jnp.dot(padded, wt[:, cols], preferred_element_type=F32)[:R]
+                xj = xs[m, j].astype(F32)
+                dy = ys[m, j].astype(F32) + rinv * (dn * gain[:, cols] - xj * pull)
+                sendb[m, j] = dy.astype(BF16)
+                if (j + 1) % EACH == 0:
+                    b_copy(m, pl.ds(j + 1 - EACH, EACH)).start()
         sib_copy(1, m).start()
 
     def forward_step(m):
@@ -203,7 +214,15 @@
         def _():
             f_copy(m, whole).wait_recv()
 
-        @pl.when(s < SECTIONS - 1)
+        @pl.when(first)
+        def _():
+            loaded(xs, m)
+
+        @pl.when(first & (m == 0))
+        def _():
+            forward(m, True, True)
+
+        @pl.when((s < SECTIONS - 1) & ((s > 0) | (m > 0)))
         def _():
             forward(m, True)
 
@@ -215,6 +234,10 @@
         @pl.when(s < SECTIONS - 1)
         def _():
             b_copy(m, whole).wait_recv()
+
+        @pl.when(last)
+        def _():
+            loaded(ys, m)
 
         @pl.when(s > 0)
         def _():
@@ -383,9 +406,12 @@
     def _():
         gram_send(0)
 
-    @pl.when(s <= 1)
+    @pl.when(s <= 3)
     def _():
         sum_gather(0)
+
+    @pl.when(s <= 2)
+    def _():
         roots(0, act_out)
 
     def second_half(i, _):
@@ -400,13 +426,13 @@
 
     gram_send(1)
 
-    @pl.when(s >= 2)
+    @pl.when(s >= 4)
     def _():
         sum_gather(0)
 
     sum_gather(1)
 
-    @pl.when(s >= 2)
+    @pl.when(s >= 3)
     def _():
         roots(0, act_out)
 
@@ -435,11 +461,17 @@
         each_peer(lambda k: ag_copy(f, k).wait_send())
 
 
+def copy_kernel(act, grad, act_out, grad_out):
+    act_out[...] = act[...]
+    grad_out[...] = grad[...]
+
+
 def shards(tokens, cotangent, gain, weight):
     out = jax.ShapeDtypeStruct((HALF, D), F32)
     dma = pltpu.SemaphoreType.DMA
     anywhere = pl.BlockSpec(memory_space=pl.ANY)
-    return pl.pallas_call(
+    chunks = (M, R, D)
+    act, grad = pl.pallas_call(
         kernel,
         out_shape=(out, out),
         in_specs=[anywhere, anywhere, pl.BlockSpec(memory_space=pltpu.VMEM), anywhere],
@@ -447,10 +479,10 @@
         scratch_shapes=[
             pltpu.VMEM((D, D), BF16),
             pltpu.VMEM((D, D), BF16),
-            pltpu.VMEM((NT, ROWS, TN), BF16),
-            pltpu.VMEM((NT, ROWS, TN), BF16),
-            pltpu.VMEM((NT, ROWS, TN), BF16),
-            pltpu.VMEM((NT, ROWS, TN), BF16),
+            pltpu.VMEM((M, NT, R, TN), BF16),
+            pltpu.VMEM((M, NT, R, TN), BF16),
+            pltpu.VMEM((M, NT, R, TN), BF16),
+            pltpu.VMEM((M, NT, R, TN), BF16),
             pltpu.VMEM((ROWS, D), F32),
             pltpu.VMEM((ROWS, D), BF16),
             pltpu.VMEM((ROWS, D), BF16),
@@ -462,8 +494,9 @@
             pltpu.VMEM((BLK, BLK), BF16),
             pltpu.VMEM((2, SLAB, BLK), F32),
             pltpu.VMEM((2, SLAB, BLK), F32),
+            pltpu.VMEM((2, PAD, D), BF16),
             dma((NT,)),
-            dma((2 * NT,)),
+            dma((2,)),
             dma((M,)),
             dma((M,)),
             dma((M,)),
@@ -482,7 +515,12 @@
         compiler_params=pltpu.CompilerParams(
             collective_id=0, has_side_effects=True, vmem_limit_bytes=58 * 2**20
         ),
-    )(tokens, cotangent, gain, weight)
+    )(tokens.reshape(chunks), cotangent.reshape(chunks), gain, weight)
+    return pl.pallas_call(
+        copy_kernel,
+        out_shape=(out, out),
+        name="results",
+    )(act, grad)
 
 
 def solution(mesh):

time: 183 us -> 155 us (0.85)
  Pallas kernels: 177 us -> 154 us
  local copies, waits for them, and re-layouts: 3.74 us -> 0 us
    pallas_call x1, Pallas kernels: 177 us -> 152 us  [shards(): pl.pallas_call(kernel, out_shape=(out, out), in_specs=[anywhere, anywhere...]
    unnamed x2 -> x0, local copies, waits for them, and re-layouts: 3.74 us -> none
    pallas_call x0 -> x1, Pallas kernels: none -> 2.2 us  [shards(): pl.pallas_call(copy_kernel, out_shape=(out, out), name='results')(act, grad)]
where the time goes in v2:
time: 155 us
  Pallas kernels  154 us (99%)
    pallas_call x1, Pallas kernels, shards(): pl.pallas_call(kernel, out_shape=(out, out), in_specs=[anywhere, anywhere...  152 us

profile of v2, /device:TPU:1, one launch (start us, length us, event | category | flops | bytes accessed | tf_op | source)
XLA Modules:
  0.0 154.7 jit_solution(7256309507685872187)
XLA Ops:
  0.6 151.8 %refresh.1 = (f32[64,2048]{1,0:T(8,128)}, f32[64,2048]{1,0:T(8,128)}) custom-call(bf16[8,32,2048]{2,1,0:T(8,128)(2,1)} %bitcast.2, bf16[8,32,2048]{2,1,0:T(8,128)(2,1)} %bitcast.3, f32[1,2048]{1,0:T(1,128)} %gain.1, bf16[2048,2048]{1,0:T(8,128)(2,1)} %wgt.1), custom_call_target="tpu_custom_call" | custom-call | tf_op jit(solution)/shard_map/refresh/pallas_call | solution.py:474
  152.5 2.2 %results.1 = (f32[64,2048]{1,0:T(8,128)}, f32[64,2048]{1,0:T(8,128)}) custom-call(f32[64,2048]{1,0:T(8,128)} %get-tuple-element.4.act, f32[64,2048]{1,0:T(8,128)} %get-tuple-element.5.grad), custom_call_target="tpu_custom_call" | custom-call | tf_op jit(solution)/shard_map/results/pallas_call | solution.py:519

commit v3 on v2

--- a/solution.py
+++ b/solution.py
@@ -22,6 +22,10 @@
 SLAB = BLK // CHIPS
 HALF = SLAB // 2
 KEPT = 5
+YZ = 3
+ZY = KEPT - YZ
+EXTRA = 16
+SPLIT = EXTRA + YZ * SLAB
 ROW_TOTAL = 4096.0
 DAMPING = 4.0
 SECTIONS = 8
@@ -46,22 +50,32 @@
 
 def kernel(
     tok, cot, gain, wgt, act_out, grad_out,
-    w, wt, xs, ys, sendf, sendb, zs, ns, ds, rinvs, sib, gram, rs, ag, full, slab, ztile, lhs,
+    w, wt, xs, ys, sendf, sendb, zs, ns, ds, rinvs, sib, gram, yp, zq, ps, qs, zp, yq, ag, full, dv, slab, ztile, lhs,
     w_sem, tok_sem, f_send, f_recv, b_send, b_recv, sib_send, sib_recv,
-    rs_send, rs_recv, ag_send, ag_recv, own_sem, out_send, out_recv,
+    yp_send, yp_recv, zq_send, zq_recv, zp_send, zp_recv, yq_send, yq_recv,
+    gp_zsend, gp_ysend, gp_recv, gq_ysend, gq_zsend, gq_fsend, gq_recv, cot_send, own_sem, out_send, out_recv,
 ):
     s = lax.axis_index("section")
     d = lax.axis_index("dp")
     chip = d // 2
     core = d % 2
-    nxt = (jnp.minimum(s + 1, SECTIONS - 1), d)
-    prv = (jnp.maximum(s - 1, 0), d)
+    zc = d // 4
+    yc = (d // 2) % 2
+    flipped = zc * 4 + (1 - yc) * 2 + core
+    nxt = (jnp.minimum(s + 1, SECTIONS - 1), jnp.where(s == 3, flipped, d))
+    prv = (jnp.maximum(s - 1, 0), jnp.where(s == 4, flipped, d))
+    ypeer = (s, flipped)
     sibling = (s, chip * 2 + 1 - core)
     first = s == 0
     last = s == SECTIONS - 1
 
-    def peer(k):
-        return (s, k * 2 + core)
+    def zpeer(z):
+        return (s, z * 4 + yc * 2 + core)
+
+    def remote(src, dst, send_sem, recv_sem, device):
+        return pltpu.make_async_remote_copy(
+            src_ref=src, dst_ref=dst, send_sem=send_sem, recv_sem=recv_sem, device_id=device, device_id_type=MESH
+        )
 
     def w_copy(j):
         cols = pl.ds(j * TN, TN)
@@ -71,6 +85,15 @@
         cols = pl.ds(j * TN, TN)
         return pltpu.make_async_copy(source.at[0, :, cols], target.at[0, j], tok_sem.at[0])
 
+    def cot_copy(part, j):
+        cols = pl.ds(j * TN, TN)
+        chunk = 0 if part == 0 else slice(1, M)
+        return remote(cot.at[chunk, :, cols], ys.at[chunk, j], cot_send.at[part], tok_sem.at[part], ypeer)
+
+    def cot_whole(part):
+        chunk = ys.at[0] if part == 0 else ys.at[1:M]
+        return remote(chunk, chunk, cot_send.at[part], tok_sem.at[part], ypeer)
+
     def rest_load(source, target, j):
         cols = pl.ds(j * TN, TN)
         return pltpu.make_async_copy(source.at[1:M, :, cols], target.at[1:M, j], tok_sem.at[1])
@@ -97,28 +120,28 @@
         for j in range(NT):
             rest_load(tok, xs, j).start()
 
+    lhs[...] = jnp.zeros_like(lhs)
+
+    barrier = pltpu.get_barrier_semaphore()
+    for neighbour in [sibling, ypeer] + [zpeer((zc + i) % 4) for i in range(1, 4)]:
+        pl.semaphore_signal(barrier, inc=1, device_id=neighbour, device_id_type=MESH)
+
+    @pl.when(s < SECTIONS - 1)
+    def _():
+        pl.semaphore_signal(barrier, inc=1, device_id=nxt, device_id_type=MESH)
+
+    @pl.when(s > 0)
+    def _():
+        pl.semaphore_signal(barrier, inc=1, device_id=prv, device_id_type=MESH)
+
+    pl.semaphore_wait(barrier, 5 + jnp.where(first, 0, 1) + jnp.where(last, 0, 1))
+
     @pl.when(last)
     def _():
         for j in range(NT):
-            first_load(cot, ys, j).start()
-            rest_load(cot, ys, j).start()
-
-    lhs[...] = jnp.zeros_like(lhs)
-
-    barrier = pltpu.get_barrier_semaphore()
-    for k in range(1, CHIPS):
-        pl.semaphore_signal(barrier, inc=1, device_id=peer((chip + k) % CHIPS), device_id_type=MESH)
-    pl.semaphore_signal(barrier, inc=1, device_id=sibling, device_id_type=MESH)
-
-    @pl.when(s < SECTIONS - 1)
-    def _():
-        pl.semaphore_signal(barrier, inc=1, device_id=nxt, device_id_type=MESH)
-
-    @pl.when(s > 0)
-    def _():
-        pl.semaphore_signal(barrier, inc=1, device_id=prv, device_id_type=MESH)
-
-    pl.semaphore_wait(barrier, CHIPS + jnp.where(first, 0, 1) + jnp.where(last, 0, 1))
+            cot_copy(0, j).start()
+        for j in range(NT):
+            cot_copy(1, j).start()
 
     @pl.when(s > 0)
     def _():
@@ -235,9 +258,13 @@
         def _():
             b_copy(m, whole).wait_recv()
 
-        @pl.when(last)
-        def _():
-            loaded(ys, m)
+        @pl.when(last & (m == 0))
+        def _():
+            cot_whole(0).wait_recv()
+
+        @pl.when(last & (m == 1))
+        def _():
+            cot_whole(1).wait_recv()
 
         @pl.when(s > 0)
         def _():
@@ -247,37 +274,58 @@
         def _():
             backward(m, False)
 
-    def rs_copy(f, k):
-        return pltpu.make_async_remote_copy(
-            src_ref=gram.at[f, pl.ds(k, KEPT), pl.ds(pl.multiple_of(k * SLAB, SLAB), SLAB), :],
-            dst_ref=rs.at[f, chip],
-            send_sem=rs_send.at[f, k], recv_sem=rs_recv.at[f, chip], device_id=peer(k), device_id_type=MESH,
-        )
-
-    def rs_arrival(f, k):
-        return pltpu.make_async_remote_copy(
-            src_ref=rs.at[f, k], dst_ref=rs.at[f, k],
-            send_sem=rs_send.at[f, k], recv_sem=rs_recv.at[f, k], device_id=peer(k), device_id_type=MESH,
-        )
-
-    def ag_copy(f, k):
-        return pltpu.make_async_remote_copy(
-            src_ref=ag.at[f, chip], dst_ref=ag.at[f, chip],
-            send_sem=ag_send.at[f, k], recv_sem=ag_recv.at[f, chip], device_id=peer(k), device_id_type=MESH,
-        )
-
-    def ag_arrival(f, k):
-        return pltpu.make_async_remote_copy(
-            src_ref=ag.at[f, k], dst_ref=ag.at[f, k],
-            send_sem=ag_send.at[f, k], recv_sem=ag_recv.at[f, k], device_id=peer(k), device_id_type=MESH,
-        )
-
-    def each_peer(fn):
-        def body(k, _):
-            fn((chip + k) % CHIPS)
+    def slab_of(f, k, tile, count):
+        return gram.at[f, pl.ds(k + tile, count), pl.ds(pl.multiple_of(k * SLAB, SLAB), SLAB), :]
+
+    def yp_copy(f, z):
+        src = slab_of(f, 2 * z + 1 - yc, 0, YZ)
+        return remote(src, yp.at[f, z], yp_send.at[f, z], yp_recv.at[f, z], ypeer)
+
+    def zq_copy(f, z, y):
+        src = slab_of(f, 2 * z + y, YZ, ZY)
+        return remote(src, zq.at[f, zc, y], zq_send.at[f, z, y], zq_recv.at[f, zc, y], zpeer(z))
+
+    def zq_arrival(f, z, y):
+        return remote(zq.at[f, z, y], zq.at[f, z, y], zq_send.at[f, z, y], zq_recv.at[f, z, y], zpeer(z))
+
+    def zp_copy(f, z):
+        return remote(ps.at[f, z], zp.at[f, zc], zp_send.at[f, z], zp_recv.at[f, zc], zpeer(z))
+
+    def zp_arrival(f, z):
+        return remote(zp.at[f, z], zp.at[f, z], zp_send.at[f, z], zp_recv.at[f, z], zpeer(z))
+
+    def yq_copy(f):
+        return remote(qs.at[f], yq.at[f], yq_send.at[f], yq_recv.at[f], ypeer)
+
+    def gp_copy(f, k, send_sem, device):
+        part = ag.at[f, k, pl.ds(0, SPLIT), :]
+        return remote(part, part, send_sem, gp_recv.at[f, k], device)
+
+    def gq_copy(f, k, send_sem, device):
+        part = ag.at[f, k, pl.ds(SPLIT, ZY * SLAB), :]
+        return remote(part, part, send_sem, gq_recv.at[f, k], device)
+
+    def gp_z(f, z):
+        return gp_copy(f, chip, gp_zsend.at[f, z], zpeer(z))
+
+    def gp_y(f, z):
+        return gp_copy(f, 2 * z + yc, gp_ysend.at[f, z], ypeer)
+
+    def gq_y(f):
+        return gq_copy(f, chip, gq_ysend.at[f], ypeer)
+
+    def gq_z(f, z):
+        return gq_copy(f, chip, gq_zsend.at[f, z], zpeer(z))
+
+    def gq_f(f, z):
+        return gq_copy(f, 2 * zc + 1 - yc, gq_fsend.at[f, z], zpeer(z))
+
+    def other_z(fn):
+        def body(i, _):
+            fn((zc + i) % 4)
             return 0
 
-        lax.fori_loop(1, CHIPS, body, 0)
+        lax.fori_loop(1, 4, body, 0)
 
     def gram_send(f):
         def landed(m, _):
@@ -301,49 +349,107 @@
                 gram[f, t, cut, :] = tile
                 if t < KEPT - 1:
                     gram[f, t + CHIPS, cut, :] = tile
-        each_peer(lambda k: rs_copy(f, k).start())
+            yp_copy(f, q).start()
+
+            @pl.when(zc != q)
+            def _():
+                for y in range(2):
+                    zq_copy(f, q, y).start()
+
+    def mine_tile(f, k, t):
+        return gram[f, k + t, pl.ds(pl.multiple_of(k * SLAB, SLAB), SLAB), :].astype(F32)
 
     def sum_gather(f):
-        mine = pl.ds(pl.multiple_of(chip * SLAB, SLAB), SLAB)
-        rs[f, chip] = gram[f, pl.ds(chip, KEPT), mine, :]
-        each_peer(lambda k: rs_arrival(f, k).wait_recv())
+        def relay(z):
+            yp_copy(f, z).wait_recv()
+            for t in range(YZ):
+                ps[f, z, t] = (mine_tile(f, 2 * z + yc, t) + yp[f, z, t].astype(F32)).astype(BF16)
+            zp_copy(f, z).start()
+
+        other_z(relay)
+        other_z(lambda z: zq_arrival(f, z, 1 - yc).wait_recv())
+        for t in range(ZY):
+            total = mine_tile(f, 2 * zc + 1 - yc, YZ + t)
+            for i in range(1, 4):
+                total = total + zq[f, (zc + i) % 4, 1 - yc, t].astype(F32)
+            qs[f, t] = total.astype(BF16)
+        yq_copy(f).start()
+        yp_copy(f, zc).wait_recv()
+        other_z(lambda z: zq_arrival(f, z, yc).wait_recv())
+        other_z(lambda z: zp_arrival(f, z).wait_recv())
         ri = lax.broadcasted_iota(jnp.int32, (SLAB, SLAB), 0)
         ci = lax.broadcasted_iota(jnp.int32, (SLAB, SLAB), 1)
         eye = ri == ci
-        for j in range(KEPT):
-            total = rs[f, 0, j].astype(F32)
-            for k in range(1, CHIPS):
-                total = total + rs[f, k, j].astype(F32)
+
+        def put(t, total):
+            ag[f, chip, EXTRA + t * SLAB : EXTRA + (t + 1) * SLAB, :] = total.astype(BF16)
+
+        for t in range(YZ):
+            total = mine_tile(f, chip, t) + yp[f, zc, t].astype(F32)
+            for i in range(1, 4):
+                total = total + zp[f, (zc + i) % 4, t].astype(F32)
             total = total * (1.0 / ROW_TOTAL)
-            if j == 0:
+            if t == 0:
                 diag = jnp.sum(jnp.where(eye, total, 0.0), axis=0, keepdims=True) + DAMPING
                 high = diag.astype(BF16).astype(F32)
-                row = lax.broadcasted_iota(jnp.int32, (16, SLAB), 0)
+                row = lax.broadcasted_iota(jnp.int32, (EXTRA, SLAB), 0)
                 extra = jnp.where(row == 0, high, jnp.where(row == 1, diag - high, 0.0))
-                ag[f, chip, KEPT * SLAB : KEPT * SLAB + 16, :] = extra.astype(BF16)
+                ag[f, chip, 0:EXTRA, :] = extra.astype(BF16)
                 total = jnp.where(eye, 0.0, total)
-            ag[f, chip, j * SLAB : (j + 1) * SLAB, :] = total.astype(BF16)
-        each_peer(lambda k: ag_copy(f, k).start())
+            put(t, total)
+        other_z(lambda z: gp_z(f, z).start())
+        gp_y(f, zc).start()
+        yq_copy(f).wait_recv()
+        for t in range(ZY):
+            total = mine_tile(f, chip, YZ + t) + yq[f, t].astype(F32)
+            for i in range(1, 4):
+                total = total + zq[f, (zc + i) % 4, yc, t].astype(F32)
+            put(YZ + t, total * (1.0 / ROW_TOTAL))
+        gq_y(f).start()
+        other_z(lambda z: gq_z(f, z).start())
+
+    def assemble(f, k):
+        here = pl.ds(pl.multiple_of(k * SLAB, SLAB), SLAB)
+        for j in range(KEPT):
+            there = pl.ds(pl.multiple_of(((k + j) % CHIPS) * SLAB, SLAB), SLAB)
+            tile = ag[f, k, EXTRA + j * SLAB : EXTRA + (j + 1) * SLAB, :]
+            full[here, there] = tile
+            if 0 < j < KEPT - 1:
+                full[there, here] = tile.T
+        dv[:, here] = jnp.sum(ag[f, k, 0:EXTRA, :].astype(F32), axis=0, keepdims=True)
+
+    def gathered(f, k):
+        gp_copy(f, k, gp_ysend.at[f, 0], ypeer).wait_recv()
+        gq_copy(f, k, gq_ysend.at[f], ypeer).wait_recv()
 
     def roots(f, out):
-        each_peer(lambda k: ag_arrival(f, k).wait_recv())
-        pieces = []
-        for k in range(CHIPS):
-            here = slice(k * SLAB, (k + 1) * SLAB)
-            for j in range(KEPT):
-                there = (k + j) % CHIPS
-                there = slice(there * SLAB, (there + 1) * SLAB)
-                tile = ag[f, k, j * SLAB : (j + 1) * SLAB, :]
-                full[here, there] = tile
-                if 0 < j < KEPT - 1:
-                    full[there, here] = tile.T
-            extra = ag[f, k, KEPT * SLAB : KEPT * SLAB + 16, :].astype(F32)
-            pieces.append(jnp.sum(extra, axis=0, keepdims=True))
-        diag = jnp.concatenate(pieces, axis=1)
-        bound = jnp.abs(diag)
-        for k in range(CHIPS):
-            part = jnp.abs(full[k * SLAB : (k + 1) * SLAB, :].astype(F32))
-            bound = bound + jnp.sum(part, axis=0, keepdims=True)
+        across = 2 * zc + 1 - yc
+
+        def pass_on(z):
+            gp_copy(f, 2 * z + yc, gp_ysend.at[f, z], ypeer).wait_recv()
+            gp_y(f, z).start()
+
+        pass_on((zc + 1) % 4)
+        gathered(f, across)
+        other_z(lambda z: gq_f(f, z).start())
+        pass_on((zc + 3) % 4)
+        pass_on((zc + 2) % 4)
+        assemble(f, chip)
+        assemble(f, across)
+
+        def direct(z):
+            gq_copy(f, 2 * z + yc, gq_ysend.at[f], ypeer).wait_recv()
+            assemble(f, 2 * z + yc)
+
+        def indirect(z):
+            gathered(f, 2 * z + 1 - yc)
+            assemble(f, 2 * z + 1 - yc)
+
+        other_z(direct)
+        other_z(indirect)
+        diag = dv[...]
+        ones = jnp.ones((16, BLK), BF16)
+        bound = jnp.abs(diag) + jnp.dot(ones, jnp.abs(full[...]), preferred_element_type=F32)[:1]
         scale = 1.0 / jnp.max(bound, axis=1, keepdims=True)
         mine = pl.ds(pl.multiple_of(chip * SLAB, SLAB), SLAB)
         ri = lax.broadcasted_iota(jnp.int32, (SLAB, BLK), 0)
@@ -456,9 +562,28 @@
         return 0
 
     lax.fori_loop(0, M, sent, 0)
+    @pl.when(last)
+    def _():
+        cot_whole(0).wait_send()
+        cot_whole(1).wait_send()
+
     for f in range(2):
-        each_peer(lambda k: rs_copy(f, k).wait_send())
-        each_peer(lambda k: ag_copy(f, k).wait_send())
+
+        def z_sent(z):
+            zq_copy(f, z, 0).wait_send()
+            zq_copy(f, z, 1).wait_send()
+            zp_copy(f, z).wait_send()
+            gp_z(f, z).wait_send()
+            gp_y(f, z).wait_send()
+            yp_copy(f, z).wait_send()
+            gq_z(f, z).wait_send()
+            gq_f(f, z).wait_send()
+
+        other_z(z_sent)
+        yp_copy(f, zc).wait_send()
+        gp_y(f, zc).wait_send()
+        yq_copy(f).wait_send()
+        gq_y(f).wait_send()
 
 
 def copy_kernel(act, grad, act_out, grad_out):
@@ -489,9 +614,15 @@
             pltpu.VMEM((ROWS, 128), F32),
             pltpu.VMEM((2, ROWS, BLK), BF16),
             pltpu.VMEM((2, CHIPS + KEPT - 1, BLK, SLAB), BF16),
-            pltpu.VMEM((2, CHIPS, KEPT, SLAB, SLAB), BF16),
-            pltpu.VMEM((2, CHIPS, KEPT * SLAB + 16, SLAB), BF16),
+            pltpu.VMEM((2, 4, YZ, SLAB, SLAB), BF16),
+            pltpu.VMEM((2, 4, 2, ZY, SLAB, SLAB), BF16),
+            pltpu.VMEM((2, 4, YZ, SLAB, SLAB), BF16),
+            pltpu.VMEM((2, ZY, SLAB, SLAB), BF16),
+            pltpu.VMEM((2, 4, YZ, SLAB, SLAB), BF16),
+            pltpu.VMEM((2, ZY, SLAB, SLAB), BF16),
+            pltpu.VMEM((2, CHIPS, EXTRA + KEPT * SLAB, SLAB), BF16),
             pltpu.VMEM((BLK, BLK), BF16),
+            pltpu.VMEM((1, BLK), F32),
             pltpu.VMEM((2, SLAB, BLK), F32),
             pltpu.VMEM((2, SLAB, BLK), F32),
             pltpu.VMEM((2, PAD, D), BF16),
@@ -503,10 +634,22 @@
             dma((M,)),
             dma((2, M)),
             dma((2, M)),
+            dma((2, 4)),
+            dma((2, 4)),
+            dma((2, 4, 2)),
+            dma((2, 4, 2)),
+            dma((2, 4)),
+            dma((2, 4)),
+            dma((2,)),
+            dma((2,)),
+            dma((2, 4)),
+            dma((2, 4)),
             dma((2, CHIPS)),
+            dma((2,)),
+            dma((2, 4)),
+            dma((2, 4)),
             dma((2, CHIPS)),
-            dma((2, CHIPS)),
-            dma((2, CHIPS)),
+            dma((2,)),
             dma((2,)),
             dma((2,)),
             dma((2,)),

time: 155 us -> 149 us (0.961)
  Pallas kernels: 154 us -> 148 us
    pallas_call x1, Pallas kernels: 152 us -> 146 us  [shards(): pl.pallas_call(kernel, out_shape=(out, out), in_specs=[anywhere, anywhere...]
where the time goes in v3:
time: 149 us; the launch traced here: 148 us
  Pallas kernels  148 us (99%)
    pallas_call x1, Pallas kernels, shards(): pl.pallas_call(kernel, out_shape=(out, out), in_specs=[anywhere, anywhere...  146 us

profile of v3, /device:TPU:1, one launch (start us, length us, event | category | flops | bytes accessed | tf_op | source)
XLA Modules:
  0.0 148.5 jit_solution(4382227471716138056)
XLA Ops:
  0.6 145.6 %refresh.1 = (f32[64,2048]{1,0:T(8,128)}, f32[64,2048]{1,0:T(8,128)}) custom-call(bf16[8,32,2048]{2,1,0:T(8,128)(2,1)} %bitcast.2, bf16[8,32,2048]{2,1,0:T(8,128)(2,1)} %bitcast.3, f32[1,2048]{1,0:T(1,128)} %gain.1, bf16[2048,2048]{1,0:T(8,128)(2,1)} %wgt.1), custom_call_target="tpu_custom_call" | custom-call | tf_op jit(solution)/shard_map/refresh/pallas_call | solution.py:599
  146.3 2.2 %results.1 = (f32[64,2048]{1,0:T(8,128)}, f32[64,2048]{1,0:T(8,128)}) custom-call(f32[64,2048]{1,0:T(8,128)} %get-tuple-element.4.act, f32[64,2048]{1,0:T(8,128)} %get-tuple-element.5.grad), custom_call_target="tpu_custom_call" | custom-call | tf_op jit(solution)/shard_map/results/pallas_call | solution.py:662

commit v4 on v3

--- a/solution.py
+++ b/solution.py
@@ -22,7 +22,7 @@
 SLAB = BLK // CHIPS
 HALF = SLAB // 2
 KEPT = 5
-YZ = 3
+YZ = 2
 ZY = KEPT - YZ
 EXTRA = 16
 SPLIT = EXTRA + YZ * SLAB
@@ -31,7 +31,7 @@
 SECTIONS = 8
 LAG = 3
 PAD = 128
-EACH = 4
+GROUPS = ((0, 4, 2), (4, 8, 2))
 
 GELU_A = 0.7978845608028654
 GELU_B = 0.044715
@@ -50,7 +50,7 @@
 
 def kernel(
     tok, cot, gain, wgt, act_out, grad_out,
-    w, wt, xs, ys, sendf, sendb, zs, ns, ds, rinvs, sib, gram, yp, zq, ps, qs, zp, yq, ag, full, dv, slab, ztile, lhs,
+    w, wt, xs, ys, sendf, sendb, zs, slopes, ns, ds, rinvs, sib, gram, yp, zq, ps, qs, zp, yq, ag, full, dv, slab, ztile, lhs,
     w_sem, tok_sem, f_send, f_recv, b_send, b_recv, sib_send, sib_recv,
     yp_send, yp_recv, zq_send, zq_recv, zp_send, zp_recv, yq_send, yq_recv,
     gp_zsend, gp_ysend, gp_recv, gq_ysend, gq_zsend, gq_fsend, gq_recv, cot_send, own_sem, out_send, out_recv,
@@ -204,9 +204,14 @@
             zs[rows, cols] = z
             if send:
                 sendf[m, j] = (xs[m, j].astype(F32) + gelu_value(z)).astype(BF16)
-                if (j + 1) % EACH == 0:
-                    f_copy(m, pl.ds(j + 1 - EACH, EACH)).start()
+                for lo, hi, step in GROUPS:
+                    if j + 1 == hi:
+                        for part in range(lo, hi, step):
+                            f_copy(m, pl.ds(part, step)).start()
         sib_copy(0, m).start()
+        for j in range(NT):
+            cols = slice(j * TN, (j + 1) * TN)
+            slopes[rows, cols] = gelu_slope(zs[rows, cols])
 
     def backward(m, send):
         rows = chunk_rows(m)
@@ -214,7 +219,7 @@
         for j in range(NT):
             cols = slice(j * TN, (j + 1) * TN)
             z = zs[rows, cols]
-            delta = (ys[m, j].astype(F32) * gelu_slope(z)).astype(BF16)
+            delta = (ys[m, j].astype(F32) * slopes[rows, cols]).astype(BF16)
             ds[rows, cols] = delta
             lhs[1, :R, cols] = delta
             total = total + delta.astype(F32) * z
@@ -228,8 +233,10 @@
                 xj = xs[m, j].astype(F32)
                 dy = ys[m, j].astype(F32) + rinv * (dn * gain[:, cols] - xj * pull)
                 sendb[m, j] = dy.astype(BF16)
-                if (j + 1) % EACH == 0:
-                    b_copy(m, pl.ds(j + 1 - EACH, EACH)).start()
+                for lo, hi, step in GROUPS:
+                    if j + 1 == hi:
+                        for part in range(lo, hi, step):
+                            b_copy(m, pl.ds(part, step)).start()
         sib_copy(1, m).start()
 
     def forward_step(m):
@@ -338,8 +345,9 @@
         own = store[:, mine]
         other = sib[f]
         dims = (((0,), (0,)), ((), ()))
-        for q in range(BLK // 256):
-            cut = slice(q * 256, (q + 1) * 256)
+        for i in range(1, 5):
+            q = (zc + i) % 4
+            cut = pl.ds(pl.multiple_of(q * 256, 256), 256)
             own_cut = store[:, pl.ds(pl.multiple_of(core * BLK + q * 256, 256), 256)]
             part = lax.dot_general(own_cut, own, dims, preferred_element_type=F32)
             part = part + lax.dot_general(sib[f, :, cut], other, dims, preferred_element_type=F32)
@@ -350,9 +358,7 @@
                 if t < KEPT - 1:
                     gram[f, t + CHIPS, cut, :] = tile
             yp_copy(f, q).start()
-
-            @pl.when(zc != q)
-            def _():
+            if i < 4:
                 for y in range(2):
                     zq_copy(f, q, y).start()
 
@@ -522,6 +528,11 @@
 
     def second_half(i, _):
         backward_step(i)
+
+        @pl.when((s == 4) & (i == 2))
+        def _():
+            sum_gather(0)
+
         return 0
 
     lax.fori_loop(M - lag, M, second_half, 0)
@@ -532,7 +543,7 @@
 
     gram_send(1)
 
-    @pl.when(s >= 4)
+    @pl.when(s >= 5)
     def _():
         sum_gather(0)
 
@@ -586,9 +597,16 @@
         gq_y(f).wait_send()
 
 
-def copy_kernel(act, grad, act_out, grad_out):
-    act_out[...] = act[...]
-    grad_out[...] = grad[...]
+def copy_kernel(act, grad, act_out, grad_out, held, sems):
+    loads = [pltpu.make_async_copy(act, held.at[0], sems.at[0]), pltpu.make_async_copy(grad, held.at[1], sems.at[1])]
+    stores = [pltpu.make_async_copy(held.at[0], act_out, sems.at[2]), pltpu.make_async_copy(held.at[1], grad_out, sems.at[3])]
+    for cp in loads:
+        cp.start()
+    for load, store in zip(loads, stores):
+        load.wait()
+        store.start()
+    for cp in stores:
+        cp.wait()
 
 
 def shards(tokens, cotangent, gain, weight):
@@ -608,6 +626,7 @@
             pltpu.VMEM((M, NT, R, TN), BF16),
             pltpu.VMEM((M, NT, R, TN), BF16),
             pltpu.VMEM((M, NT, R, TN), BF16),
+            pltpu.VMEM((ROWS, D), F32),
             pltpu.VMEM((ROWS, D), F32),
             pltpu.VMEM((ROWS, D), BF16),
             pltpu.VMEM((ROWS, D), BF16),
@@ -662,6 +681,9 @@
     return pl.pallas_call(
         copy_kernel,
         out_shape=(out, out),
+        in_specs=[anywhere] * 2,
+        out_specs=(anywhere, anywhere),
+        scratch_shapes=[pltpu.VMEM((2, HALF, D), F32), dma((4,))],
         name="results",
     )(act, grad)
 

time: 149 us -> 147 us (0.987)
  Pallas kernels: 148 us -> 146 us
where the time goes in v4:
time: 147 us
  Pallas kernels  146 us (99%)
    pallas_call x1, Pallas kernels, shards(): pl.pallas_call(kernel, out_shape=(out, out), in_specs=[anywhere, anywhere...  144 us

profile of v4, /device:TPU:1, one launch (start us, length us, event | category | flops | bytes accessed | tf_op | source)
XLA Modules:
  0.0 147.0 jit_solution(11614180656023409011)
XLA Ops:
  0.6 144.2 %refresh.1 = (f32[64,2048]{1,0:T(8,128)}, f32[64,2048]{1,0:T(8,128)}) custom-call(bf16[8,32,2048]{2,1,0:T(8,128)(2,1)} %bitcast.2, bf16[8,32,2048]{2,1,0:T(8,128)(2,1)} %bitcast.3, f32[1,2048]{1,0:T(1,128)} %gain.1, bf16[2048,2048]{1,0:T(8,128)(2,1)} %wgt.1), custom_call_target="tpu_custom_call" | custom-call | tf_op jit(solution)/shard_map/refresh/pallas_call | solution.py:617
  144.8 2.0 %results.1 = (f32[64,2048]{1,0:T(8,128)}, f32[64,2048]{1,0:T(8,128)}) custom-call(f32[64,2048]{1,0:T(8,128)} %get-tuple-element.4.act, f32[64,2048]{1,0:T(8,128)} %get-tuple-element.5.grad), custom_call_target="tpu_custom_call" | custom-call | tf_op jit(solution)/shard_map/results/pallas_call | solution.py:681

commit v5 on v4

--- a/solution.py
+++ b/solution.py
@@ -50,9 +50,9 @@
 
 def kernel(
     tok, cot, gain, wgt, act_out, grad_out,
-    w, wt, xs, ys, sendf, sendb, zs, slopes, ns, ds, rinvs, sib, gram, yp, zq, ps, qs, zp, yq, ag, full, dv, slab, ztile, lhs,
+    w, wt, xs, ys, sendf, sendb, zs, slopes, ns, ds, rinvs, sib, gram, zp, ag, full, dv, slab, ztile, lhs,
     w_sem, tok_sem, f_send, f_recv, b_send, b_recv, sib_send, sib_recv,
-    yp_send, yp_recv, zq_send, zq_recv, zp_send, zp_recv, yq_send, yq_recv,
+    zp_send, zp_recv,
     gp_zsend, gp_ysend, gp_recv, gq_ysend, gq_zsend, gq_fsend, gq_recv, cot_send, own_sem, out_send, out_recv,
 ):
     s = lax.axis_index("section")
@@ -65,6 +65,7 @@
     nxt = (jnp.minimum(s + 1, SECTIONS - 1), jnp.where(s == 3, flipped, d))
     prv = (jnp.maximum(s - 1, 0), jnp.where(s == 4, flipped, d))
     ypeer = (s, flipped)
+    ydiag = (s, zc * 4 + (1 - yc) * 2 + 1 - core)
     sibling = (s, chip * 2 + 1 - core)
     first = s == 0
     last = s == SECTIONS - 1
@@ -123,7 +124,7 @@
     lhs[...] = jnp.zeros_like(lhs)
 
     barrier = pltpu.get_barrier_semaphore()
-    for neighbour in [sibling, ypeer] + [zpeer((zc + i) % 4) for i in range(1, 4)]:
+    for neighbour in [sibling, ypeer, ydiag] + [zpeer((zc + i) % 4) for i in range(1, 4)]:
         pl.semaphore_signal(barrier, inc=1, device_id=neighbour, device_id_type=MESH)
 
     @pl.when(s < SECTIONS - 1)
@@ -134,7 +135,7 @@
     def _():
         pl.semaphore_signal(barrier, inc=1, device_id=prv, device_id_type=MESH)
 
-    pl.semaphore_wait(barrier, 5 + jnp.where(first, 0, 1) + jnp.where(last, 0, 1))
+    pl.semaphore_wait(barrier, 6 + jnp.where(first, 0, 1) + jnp.where(last, 0, 1))
 
     @pl.when(last)
     def _():
@@ -174,13 +175,20 @@
 
     whole = pl.ds(0, NT)
 
-    def sib_copy(f, m):
+    near = (sibling, ypeer, ydiag)
+
+    def sib_copy(f, m, p):
         rows = chunk_rows(m)
         store = ns if f == 0 else ds
-        return pltpu.make_async_remote_copy(
-            src_ref=store.at[rows, pl.ds(pl.multiple_of((1 - core) * BLK, BLK), BLK)], dst_ref=sib.at[f, rows, :],
-            send_sem=sib_send.at[f, m], recv_sem=sib_recv.at[f, m], device_id=sibling, device_id_type=MESH,
+        block = core if p == 1 else 1 - core
+        return remote(
+            store.at[rows, pl.ds(pl.multiple_of(block * BLK, BLK), BLK)], sib.at[f, p, rows, :],
+            sib_send.at[f, p, m], sib_recv.at[f, p, m], near[p],
         )
+
+    def share(f, m):
+        for p in range(3):
+            sib_copy(f, m, p).start()
 
     def forward(m, send, fresh=False):
         rows = chunk_rows(m)
@@ -208,7 +216,7 @@
                     if j + 1 == hi:
                         for part in range(lo, hi, step):
                             f_copy(m, pl.ds(part, step)).start()
-        sib_copy(0, m).start()
+        share(0, m)
         for j in range(NT):
             cols = slice(j * TN, (j + 1) * TN)
             slopes[rows, cols] = gelu_slope(zs[rows, cols])
@@ -237,7 +245,7 @@
                     if j + 1 == hi:
                         for part in range(lo, hi, step):
                             b_copy(m, pl.ds(part, step)).start()
-        sib_copy(1, m).start()
+        share(1, m)
 
     def forward_step(m):
         @pl.when(s > 0)
@@ -284,25 +292,12 @@
     def slab_of(f, k, tile, count):
         return gram.at[f, pl.ds(k + tile, count), pl.ds(pl.multiple_of(k * SLAB, SLAB), SLAB), :]
 
-    def yp_copy(f, z):
-        src = slab_of(f, 2 * z + 1 - yc, 0, YZ)
-        return remote(src, yp.at[f, z], yp_send.at[f, z], yp_recv.at[f, z], ypeer)
-
-    def zq_copy(f, z, y):
-        src = slab_of(f, 2 * z + y, YZ, ZY)
-        return remote(src, zq.at[f, zc, y], zq_send.at[f, z, y], zq_recv.at[f, zc, y], zpeer(z))
-
-    def zq_arrival(f, z, y):
-        return remote(zq.at[f, z, y], zq.at[f, z, y], zq_send.at[f, z, y], zq_recv.at[f, z, y], zpeer(z))
-
     def zp_copy(f, z):
-        return remote(ps.at[f, z], zp.at[f, zc], zp_send.at[f, z], zp_recv.at[f, zc], zpeer(z))
+        src = slab_of(f, 2 * z + yc, 0, KEPT)
+        return remote(src, zp.at[f, zc], zp_send.at[f, z], zp_recv.at[f, zc], zpeer(z))
 
     def zp_arrival(f, z):
         return remote(zp.at[f, z], zp.at[f, z], zp_send.at[f, z], zp_recv.at[f, z], zpeer(z))
-
-    def yq_copy(f):
-        return remote(qs.at[f], yq.at[f], yq_send.at[f], yq_recv.at[f], ypeer)
 
     def gp_copy(f, k, send_sem, device):
         part = ag.at[f, k, pl.ds(0, SPLIT), :]
@@ -336,52 +331,35 @@
 
     def gram_send(f):
         def landed(m, _):
-            sib_copy(f, m).wait_recv()
+            for p in range(3):
+                sib_copy(f, m, p).wait_recv()
             return 0
 
         lax.fori_loop(0, M, landed, 0)
         store = ns if f == 0 else ds
-        mine = pl.ds(pl.multiple_of(core * BLK, BLK), BLK)
-        own = store[:, mine]
-        other = sib[f]
+        own = store[:, pl.ds(pl.multiple_of(core * BLK, BLK), BLK)]
         dims = (((0,), (0,)), ((), ()))
         for i in range(1, 5):
             q = (zc + i) % 4
-            cut = pl.ds(pl.multiple_of(q * 256, 256), 256)
-            own_cut = store[:, pl.ds(pl.multiple_of(core * BLK + q * 256, 256), 256)]
+            k = 2 * q + yc
+            cut = pl.ds(pl.multiple_of(k * SLAB, SLAB), SLAB)
+            own_cut = store[:, pl.ds(pl.multiple_of(core * BLK + k * SLAB, SLAB), SLAB)]
             part = lax.dot_general(own_cut, own, dims, preferred_element_type=F32)
-            part = part + lax.dot_general(sib[f, :, cut], other, dims, preferred_element_type=F32)
+            for p in range(3):
+                part = part + lax.dot_general(sib[f, p, :, cut], sib[f, p], dims, preferred_element_type=F32)
             part = part.astype(BF16)
             for t in range(CHIPS):
                 tile = part[:, t * SLAB : (t + 1) * SLAB]
                 gram[f, t, cut, :] = tile
                 if t < KEPT - 1:
                     gram[f, t + CHIPS, cut, :] = tile
-            yp_copy(f, q).start()
             if i < 4:
-                for y in range(2):
-                    zq_copy(f, q, y).start()
+                zp_copy(f, q).start()
 
     def mine_tile(f, k, t):
         return gram[f, k + t, pl.ds(pl.multiple_of(k * SLAB, SLAB), SLAB), :].astype(F32)
 
     def sum_gather(f):
-        def relay(z):
-            yp_copy(f, z).wait_recv()
-            for t in range(YZ):
-                ps[f, z, t] = (mine_tile(f, 2 * z + yc, t) + yp[f, z, t].astype(F32)).astype(BF16)
-            zp_copy(f, z).start()
-
-        other_z(relay)
-        other_z(lambda z: zq_arrival(f, z, 1 - yc).wait_recv())
-        for t in range(ZY):
-            total = mine_tile(f, 2 * zc + 1 - yc, YZ + t)
-            for i in range(1, 4):
-                total = total + zq[f, (zc + i) % 4, 1 - yc, t].astype(F32)
-            qs[f, t] = total.astype(BF16)
-        yq_copy(f).start()
-        yp_copy(f, zc).wait_recv()
-        other_z(lambda z: zq_arrival(f, z, yc).wait_recv())
         other_z(lambda z: zp_arrival(f, z).wait_recv())
         ri = lax.broadcasted_iota(jnp.int32, (SLAB, SLAB), 0)
         ci = lax.broadcasted_iota(jnp.int32, (SLAB, SLAB), 1)
@@ -390,8 +368,8 @@
         def put(t, total):
             ag[f, chip, EXTRA + t * SLAB : EXTRA + (t + 1) * SLAB, :] = total.astype(BF16)
 
-        for t in range(YZ):
-            total = mine_tile(f, chip, t) + yp[f, zc, t].astype(F32)
+        for t in range(KEPT):
+            total = mine_tile(f, chip, t)
             for i in range(1, 4):
                 total = total + zp[f, (zc + i) % 4, t].astype(F32)
             total = total * (1.0 / ROW_TOTAL)
@@ -402,15 +380,10 @@
                 extra = jnp.where(row == 0, high, jnp.where(row == 1, diag - high, 0.0))
                 ag[f, chip, 0:EXTRA, :] = extra.astype(BF16)
                 total = jnp.where(eye, 0.0, total)
-            put(t, total)
-        other_z(lambda z: gp_z(f, z).start())
-        gp_y(f, zc).start()
-        yq_copy(f).wait_recv()
-        for t in range(ZY):
-            total = mine_tile(f, chip, YZ + t) + yq[f, t].astype(F32)
-            for i in range(1, 4):
-                total = total + zq[f, (zc + i) % 4, yc, t].astype(F32)
-            put(YZ + t, total * (1.0 / ROW_TOTAL))
+            ag[f, chip, EXTRA + t * SLAB : EXTRA + (t + 1) * SLAB, :] = total.astype(BF16)
+            if t == YZ - 1:
+                other_z(lambda z: gp_z(f, z).start())
+                gp_y(f, zc).start()
         gq_y(f).start()
         other_z(lambda z: gq_z(f, z).start())
 
@@ -568,8 +541,9 @@
         def _():
             b_copy(m, whole).wait_send()
 
-        sib_copy(0, m).wait_send()
-        sib_copy(1, m).wait_send()
+        for p in range(3):
+            sib_copy(0, m, p).wait_send()
+            sib_copy(1, m, p).wait_send()
         return 0
 
     lax.fori_loop(0, M, sent, 0)
@@ -581,19 +555,14 @@
     for f in range(2):
 
         def z_sent(z):
-            zq_copy(f, z, 0).wait_send()
-            zq_copy(f, z, 1).wait_send()
             zp_copy(f, z).wait_send()
             gp_z(f, z).wait_send()
             gp_y(f, z).wait_send()
-            yp_copy(f, z).wait_send()
             gq_z(f, z).wait_send()
             gq_f(f, z).wait_send()
 
         other_z(z_sent)
-        yp_copy(f, zc).wait_send()
         gp_y(f, zc).wait_send()
-        yq_copy(f).wait_send()
         gq_y(f).wait_send()
 
 
@@ -631,14 +600,9 @@
             pltpu.VMEM((ROWS, D), BF16),
             pltpu.VMEM((ROWS, D), BF16),
             pltpu.VMEM((ROWS, 128), F32),
-            pltpu.VMEM((2, ROWS, BLK), BF16),
+            pltpu.VMEM((2, 3, ROWS, BLK), BF16),
             pltpu.VMEM((2, CHIPS + KEPT - 1, BLK, SLAB), BF16),
-            pltpu.VMEM((2, 4, YZ, SLAB, SLAB), BF16),
-            pltpu.VMEM((2, 4, 2, ZY, SLAB, SLAB), BF16),
-            pltpu.VMEM((2, 4, YZ, SLAB, SLAB), BF16),
-            pltpu.VMEM((2, ZY, SLAB, SLAB), BF16),
-            pltpu.VMEM((2, 4, YZ, SLAB, SLAB), BF16),
-            pltpu.VMEM((2, ZY, SLAB, SLAB), BF16),
+            pltpu.VMEM((2, 4, KEPT, SLAB, SLAB), BF16),
             pltpu.VMEM((2, CHIPS, EXTRA + KEPT * SLAB, SLAB), BF16),
             pltpu.VMEM((BLK, BLK), BF16),
             pltpu.VMEM((1, BLK), F32),
@@ -651,16 +615,10 @@
             dma((M,)),
             dma((M,)),
             dma((M,)),
-            dma((2, M)),
-            dma((2, M)),
+            dma((2, 3, M)),
+            dma((2, 3, M)),
             dma((2, 4)),
             dma((2, 4)),
-            dma((2, 4, 2)),
-            dma((2, 4, 2)),
-            dma((2, 4)),
-            dma((2, 4)),
-            dma((2,)),
-            dma((2,)),
             dma((2, 4)),
             dma((2, 4)),
             dma((2, CHIPS)),

time: 147 us -> 146 us (level)
    pallas_call x1, Pallas kernels: 144 us -> 143 us  [shards(): pl.pallas_call(kernel, out_shape=(out, out), in_specs=[anywhere, anywhere...]
where the time goes in v5:
time: 146 us; the launch traced here: 145 us
  Pallas kernels  145 us (99%)
    pallas_call x1, Pallas kernels, shards(): pl.pallas_call(kernel, out_shape=(out, out), in_specs=[anywhere, anywhere...  143 us

profile of v5, /device:TPU:1, one launch (start us, length us, event | category | flops | bytes accessed | tf_op | source)
XLA Modules:
  0.0 145.4 jit_solution(519622966590080459)
XLA Ops:
  0.6 142.5 %refresh.1 = (f32[64,2048]{1,0:T(8,128)}, f32[64,2048]{1,0:T(8,128)}) custom-call(bf16[8,32,2048]{2,1,0:T(8,128)(2,1)} %bitcast.2, bf16[8,32,2048]{2,1,0:T(8,128)(2,1)} %bitcast.3, f32[1,2048]{1,0:T(1,128)} %gain.1, bf16[2048,2048]{1,0:T(8,128)(2,1)} %wgt.1), custom_call_target="tpu_custom_call" | custom-call | tf_op jit(solution)/shard_map/refresh/pallas_call | solution.py:586
  143.2 2.0 %results.1 = (f32[64,2048]{1,0:T(8,128)}, f32[64,2048]{1,0:T(8,128)}) custom-call(f32[64,2048]{1,0:T(8,128)} %get-tuple-element.4.act, f32[64,2048]{1,0:T(8,128)} %get-tuple-element.5.grad), custom_call_target="tpu_custom_call" | custom-call | tf_op jit(solution)/shard_map/results/pallas_call | solution.py:639

commit v6 on v5

--- a/solution.py
+++ b/solution.py
@@ -50,7 +50,7 @@
 
 def kernel(
     tok, cot, gain, wgt, act_out, grad_out,
-    w, wt, xs, ys, sendf, sendb, zs, slopes, ns, ds, rinvs, sib, gram, zp, ag, full, dv, slab, ztile, lhs,
+    w, wt, xs, ys, sendf, sendb, zs, slopes, ns, ds, rinvs, sib, partial, gram, zp, ag, full, dv, slab, ztile, lhs,
     w_sem, tok_sem, f_send, f_recv, b_send, b_recv, sib_send, sib_recv,
     zp_send, zp_recv,
     gp_zsend, gp_ysend, gp_recv, gq_ysend, gq_zsend, gq_fsend, gq_recv, cot_send, own_sem, out_send, out_recv,
@@ -187,7 +187,7 @@
         )
 
     def share(f, m):
-        for p in range(3):
+        for p in (1, 2, 0):
             sib_copy(f, m, p).start()
 
     def forward(m, send, fresh=False):
@@ -335,18 +335,32 @@
                 sib_copy(f, m, p).wait_recv()
             return 0
 
-        lax.fori_loop(0, M, landed, 0)
+        lax.fori_loop(0, M - 1, landed, 0)
+        sib_copy(f, M - 1, 0).wait_recv()
+        early = ROWS - R
         store = ns if f == 0 else ds
         own = store[:, pl.ds(pl.multiple_of(core * BLK, BLK), BLK)]
         dims = (((0,), (0,)), ((), ()))
         for i in range(1, 5):
+            k = 2 * ((zc + i) % 4) + yc
+            cut = pl.ds(pl.multiple_of(k * SLAB, SLAB), SLAB)
+            own_cut = store[:, pl.ds(pl.multiple_of(core * BLK + k * SLAB, SLAB), SLAB)]
+            part = lax.dot_general(own_cut, own, dims, preferred_element_type=F32)
+            part = part + lax.dot_general(sib[f, 0, :, cut], sib[f, 0], dims, preferred_element_type=F32)
+            for p in (1, 2):
+                part = part + lax.dot_general(
+                    sib[f, p, :early, cut], sib[f, p, :early, :], dims, preferred_element_type=F32
+                )
+            partial[i - 1] = part
+        for p in (1, 2):
+            sib_copy(f, M - 1, p).wait_recv()
+        rest = jnp.concatenate([sib[f, 1, early:, :], sib[f, 2, early:, :]], axis=0)
+        for i in range(1, 5):
             q = (zc + i) % 4
             k = 2 * q + yc
             cut = pl.ds(pl.multiple_of(k * SLAB, SLAB), SLAB)
-            own_cut = store[:, pl.ds(pl.multiple_of(core * BLK + k * SLAB, SLAB), SLAB)]
-            part = lax.dot_general(own_cut, own, dims, preferred_element_type=F32)
-            for p in range(3):
-                part = part + lax.dot_general(sib[f, p, :, cut], sib[f, p], dims, preferred_element_type=F32)
+            rest_cut = jnp.concatenate([sib[f, 1, early:, cut], sib[f, 2, early:, cut]], axis=0)
+            part = partial[i - 1] + lax.dot_general(rest_cut, rest, dims, preferred_element_type=F32)
             part = part.astype(BF16)
             for t in range(CHIPS):
                 tile = part[:, t * SLAB : (t + 1) * SLAB]
@@ -601,6 +615,7 @@
             pltpu.VMEM((ROWS, D), BF16),
             pltpu.VMEM((ROWS, 128), F32),
             pltpu.VMEM((2, 3, ROWS, BLK), BF16),
+            pltpu.VMEM((4, SLAB, BLK), F32),
             pltpu.VMEM((2, CHIPS + KEPT - 1, BLK, SLAB), BF16),
             pltpu.VMEM((2, 4, KEPT, SLAB, SLAB), BF16),
             pltpu.VMEM((2, CHIPS, EXTRA + KEPT * SLAB, SLAB), BF16),

time: 146 us -> 145 us (level)
  no operation moved by 1% of the time
where the time goes in v6:
time: 145 us
  Pallas kernels  144 us (99%)
    pallas_call x1, Pallas kernels, shards(): pl.pallas_call(kernel, out_shape=(out, out), in_specs=[anywhere, anywhere...  142 us

profile of v6, /device:TPU:1, one launch (start us, length us, event | category | flops | bytes accessed | tf_op | source)
XLA Modules:
  0.0 144.7 jit_solution(16413109354384832564)
XLA Ops:
  0.6 141.9 %refresh.1 = (f32[64,2048]{1,0:T(8,128)}, f32[64,2048]{1,0:T(8,128)}) custom-call(bf16[8,32,2048]{2,1,0:T(8,128)(2,1)} %bitcast.2, bf16[8,32,2048]{2,1,0:T(8,128)(2,1)} %bitcast.3, f32[1,2048]{1,0:T(1,128)} %gain.1, bf16[2048,2048]{1,0:T(8,128)(2,1)} %wgt.1), custom_call_target="tpu_custom_call" | custom-call | tf_op jit(solution)/shard_map/refresh/pallas_call | solution.py:600
  142.5 2.0 %results.1 = (f32[64,2048]{1,0:T(8,128)}, f32[64,2048]{1,0:T(8,128)}) custom-call(f32[64,2048]{1,0:T(8,128)} %get-tuple-element.4.act, f32[64,2048]{1,0:T(8,128)} %get-tuple-element.5.grad), custom_call_target="tpu_custom_call" | custom-call | tf_op jit(solution)/shard_map/results/pallas_call | solution.py:654
